TPU v7x, 256 devices: a whole 4x4x8 slice. The times are simulated.
256 devices in a mesh: req: 8 (over y, z_hi), tp: 32 (over z_lo, x, core).
Axes of the slice: x: 4, y: 4, z: 8 (z_hi: 2, z_lo: 4; z = z_hi * 4 + z_lo), core: 2. Of those that a mesh axis runs over, the one named last changes fastest.
Arguments:
- tokens: bfloat16 [2048, 4096], P('req', 'tp'), parts along dimension 0, may hold values from -6 to 6
- gate_codes: int32 [1024, 28672], P(None, 'tp'), may hold values from -32768 to 32767, as said below
- gate_scales: bfloat16 [32, 28672], P(None, 'tp'), as said below
- up_codes: int32 [1024, 28672], P(None, 'tp'), may hold values from -32768 to 32767, as said below
- up_scales: bfloat16 [32, 28672], P(None, 'tp'), as said below
- local_factor: bfloat16 [896, 896], replicated, may hold values from -0.1875 to 0.1875
- down_codes: int32 [7168, 4096], P('tp'), may hold values from -32768 to 32767, as said below
- down_scales: bfloat16 [224, 4096], P('tp'), as said below
Outputs:
- mixed: bfloat16 [2048, 4096], P('req', 'tp'), parts along dimension 0
There are 8 independent parts, one for each index of `req`. A program takes and returns all parts, laid end to end along the dimension named above; an argument that names none is the same for every part. Nothing has to cross between parts.
Inputs may be any that keep to these rules, and one draw needn't show every extreme that they name: `gate_codes`: each word plus 32768 holds four 4-bit codes; field k (bits 4k to 4k+3, read as 0 to 15) of word r belongs to weight row 4r+k. `up_codes`: each word plus 32768 holds four 4-bit codes; field k of word r belongs to weight row 4r+k. `down_codes`: each word plus 32768 holds four 4-bit codes; field k of word r belongs to hidden unit 4r+k. `gate_scales`: Positive. `up_scales`: Positive. `down_scales`: Positive.
All inputs are finite; a program needn't handle non-finite values.
Results may differ from a plain program's by a relative error of at most 0.034.
Values may be sent and summed in bfloat16 or wider, within the bound.
A program may use at most 128 MiB of HBM per device.

v0:
```python
import math

import jax
import jax.numpy as jnp
from jax import lax
from jax.sharding import PartitionSpec as P


def from_partner(value, axis, apart):
    mask = 2**apart
    pairs = [(source, source ^ mask) for source in range(lax.axis_size(axis))]
    return lax.ppermute(value, axis, pairs)


def unpack(packed, scales):
    row_count = packed.shape[0] * 4
    col_count = packed.shape[1]
    groups = scales.shape[0]
    shifts = (4 * jnp.arange(4, dtype=jnp.int32))[None, :, None]
    lifted = packed + 32768
    nibble = jnp.bitwise_and(jnp.right_shift(lifted[:, None, :], shifts), 15)
    values = (nibble - 8).astype(jnp.float32).reshape(groups, row_count // groups, col_count)
    values = values * scales.astype(jnp.float32)[:, None, :]
    return values.reshape(row_count, col_count).astype(jnp.bfloat16)


def shards(
    tokens, gate_codes, gate_scales, up_codes, up_scales, local_factor, down_codes, down_scales
):
    unit_count = gate_codes.shape[1]
    w_both = jnp.concatenate([unpack(gate_codes, gate_scales), unpack(up_codes, up_scales)], axis=1)
    gate_up = jnp.dot(
        lax.all_gather(tokens, "tp", axis=1, tiled=True), w_both, preferred_element_type=jnp.float32
    )
    hidden = (jax.nn.silu(gate_up[:, :unit_count]) * gate_up[:, unit_count:]).astype(jnp.bfloat16)
    blocked = jnp.dot(hidden, local_factor, preferred_element_type=jnp.float32).astype(jnp.bfloat16)
    devices = lax.axis_size("tp")
    levels = devices.bit_length() - 1
    factor = 1.0 / math.sqrt(devices)
    current = blocked.astype(jnp.float32)
    position = lax.axis_index("tp")
    section_bits = list(range(levels))
    for section in section_bits:
        partner = from_partner(current.astype(jnp.bfloat16), "tp", section).astype(current.dtype)
        is_upper = jnp.bitwise_and(jnp.right_shift(position, section), 1) == 1
        current = jnp.where(is_upper, partner - current, partner + current)
    rotated = (current * factor).astype(jnp.bfloat16)
    w_down = unpack(down_codes, down_scales)
    partial_value = jnp.dot(rotated, w_down, preferred_element_type=jnp.float32)
    return lax.psum_scatter(
        partial_value.astype(jnp.bfloat16), "tp", scatter_dimension=1, tiled=True
    )


def solution(mesh):
    return jax.shard_map(
        shards,
        mesh=mesh,
        in_specs=(
            P("req", "tp"),
            P(None, "tp"),
            P(None, "tp"),
            P(None, "tp"),
            P(None, "tp"),
            P(),
            P("tp", None),
            P("tp", None),
        ),
        out_specs=P("req", "tp"),
        check_vma=False,
    )
```

profile of v0, /device:TPU:16, one launch (start us, length us, event | category | flops | bytes accessed | tf_op | source)
XLA Modules:
  0.0 342.7 jit_solution(14981334321401842786)
XLA Ops:
  6.5 0.7 all-gather.2.cloned.1.call-update
  7.3 0.1 shift_right_arithmetic.98
  7.4 2.3 broadcast_add_fusion.1
  9.7 7.1 %shift_right_arithmetic.103 = s32[1024,4,896]{2,1,0:T(4,128)} broadcast(s32[1024,896]{1,0:T(8,128)S(1)} %broadcast_add_fusion.1), dimensions={0,2} | broadcast | bytes 18350080 | tf_op jit(solution)/shard_map/shift_right_arithmetic | solution.py:21
  16.8 17.2 %shift_right_arithmetic.104 = s32[4096,896]{1,0:T(8,128)} reshape(s32[1024,4,896]{2,1,0:T(4,128)} %shift_right_arithmetic.103) | data formatting | bytes 29360128 | tf_op jit(solution)/shard_map/shift_right_arithmetic | solution.py:21
  34.0 2.3 broadcast_add_fusion.2
  36.3 7.1 %shift_right_arithmetic.95 = s32[1024,4,896]{2,1,0:T(4,128)} broadcast(s32[1024,896]{1,0:T(8,128)S(1)} %broadcast_add_fusion.2), dimensions={0,2} | broadcast | bytes 18350080 | tf_op jit(solution)/shard_map/shift_right_arithmetic | solution.py:21
  43.4 17.2 %shift_right_arithmetic.96 = s32[4096,896]{1,0:T(8,128)} reshape(s32[1024,4,896]{2,1,0:T(4,128)} %shift_right_arithmetic.95) | data formatting | bytes 29360128 | tf_op jit(solution)/shard_map/shift_right_arithmetic | solution.py:21
  60.7 15.8 %fusion.6 = (bf16[4096,896]{1,0:T(8,128)(2,1)}, bf16[4096,896]{1,0:T(8,128)(2,1)}) fusion(s32[4096,896]{1,0:T(8,128)} %shift_right_arithmetic.96, f32[32,896]{1,0:T(8,128)S(1)} %convert_element_type.77, s32[4096]{0:T(1024)S(1)} %broadcast_bitcast_fusion, f32[32,896]{1,0:T(8,128)S(1)} %convert_element_type.80, s32[4096,896]{1,0:T(8,128)} %shift_right_arithmetic.104), kind=kLoop, calls=%fused_computation.9 | loop fusion | flops 44040192 | bytes 44285952 | tf_op jit(solution)/shard_map/convert_element_type | solution.py:24
  76.5 10.0 %fusion.7 = f32[256,1792]{0,1:T(8,128)S(1)} fusion(bf16[256,4096]{1,0:T(8,128)(2,1)} %all-gather.2.cloned.1.call-done, bf16[4096,896]{1,0:T(8,128)(2,1)} %get-tuple-element.8, bf16[4096,896]{1,0:T(8,128)(2,1)} %get-tuple-element.7), kind=kOutput, calls=%fused_computation.11 | convolution fusion | flops 3787456512 | bytes 18612224 | tf_op jit(solution)/shard_map/dot_general | solution.py:32
  86.5 0.8 convolution_convert_fusion.1
  87.3 0.1 collective-permute-start
  87.4 1.8 collective-permute-done
  89.2 0.2 fusion.18
  89.3 1.5 collective-permute-start.1
  90.9 11.1 %collective-permute-done.1 = bf16[256,896]{1,0:T(8,128)(2,1)S(1)} collective-permute-done((bf16[256,896]{1,0:T(8,128)(2,1)S(1)}, bf16[256,896]{1,0:T(8,128)(2,1)S(1)}, u32[]{:S(2)}, u32[]{:S(2)}) %collective-permute-start.1) | collective-permute-done | bytes 458784 | tf_op jit(solution)/shard_map/ppermute | solution.py:12
  102.0 0.3 fusion.26
  102.3 3.2 collective-permute-start.2
  105.5 10.4 %collective-permute-done.2 = bf16[256,896]{1,0:T(8,128)(2,1)} collective-permute-done((bf16[256,896]{1,0:T(8,128)(2,1)S(1)}, bf16[256,896]{1,0:T(8,128)(2,1)}, u32[]{:S(2)}, u32[]{:S(2)}) %collective-permute-start.2) | collective-permute-done | bytes 458784 | tf_op jit(solution)/shard_map/ppermute | solution.py:12
  115.9 2.4 fusion.30
  118.3 1.8 collective-permute-start.3
  120.1 9.3 %collective-permute-done.3 = bf16[256,896]{1,0:T(8,128)(2,1)S(1)} collective-permute-done((bf16[256,896]{1,0:T(8,128)(2,1)}, bf16[256,896]{1,0:T(8,128)(2,1)S(1)}, u32[]{:S(2)}, u32[]{:S(2)}) %collective-permute-start.3) | collective-permute-done | bytes 458784 | tf_op jit(solution)/shard_map/ppermute | solution.py:12
  129.4 0.9 fusion.19
  130.3 3.2 collective-permute-start.4
  133.5 4.2 %broadcast_add_fusion = s32[224,4096]{1,0:T(8,128)} fusion(s32[224,4096]{1,0:T(8,128)} %param.14), kind=kLoop, calls=%fused_computation.12 | loop fusion | flops 917504 | bytes 7340032 | tf_op jit(solution)/shard_map/add | solution.py:20
  137.8 9.4 %shift_right_arithmetic.106 = s32[224,4,4096]{2,1,0:T(4,128)} broadcast(s32[224,4096]{1,0:T(8,128)} %broadcast_add_fusion), dimensions={0,2} | broadcast | bytes 18350080 | tf_op jit(solution)/shard_map/shift_right_arithmetic | solution.py:21
  147.1 17.1 %shift_right_arithmetic.107 = s32[896,4096]{1,0:T(8,128)} reshape(s32[224,4,4096]{2,1,0:T(4,128)} %shift_right_arithmetic.106) | data formatting | bytes 29360128 | tf_op jit(solution)/shard_map/shift_right_arithmetic | solution.py:21
  164.3 11.4 %fusion.4 = bf16[896,4096]{1,0:T(8,128)(2,1)} fusion(s32[896,4096]{1,0:T(8,128)} %shift_right_arithmetic.107, f32[7,4096]{1,0:T(8,128)S(1)} %convert_element_type.96, s32[896]{0:T(1024)S(1)} %broadcast_bitcast_fusion.1), kind=kLoop, calls=%fused_computation.5 | loop fusion | flops 22020096 | bytes 22138368 | tf_op jit(solution)/shard_map/convert_element_type | solution.py:24
  175.7 7.0 %convolution_convert_fusion = bf16[256,4096]{1,0:T(8,128)(2,1)} fusion(bf16[896,4096]{1,0:T(8,128)(2,1)} %fusion.4, bf16[256,896]{1,0:T(8,128)(2,1)} %collective-permute-done.4, f32[256,896]{1,0:T(8,128)S(1)} %get-tuple-element.6, bf16[256,896]{1,0:T(8,128)(2,1)S(1)} %collective-permute-done.3, pred[]{:T(512)S(6)} %eq.16, pred[]{:T(512)S(6)} %eq.15), kind=kOutput, calls=%fused_computation.10 | convolution fusion | flops 1882390528 | bytes 11272194 | tf_op jit(solution)/shard_map/dot_general | solution.py:49
  182.7 4.1 %copy.9 = bf16[256,4096]{0,1:T(8,128)(2,1)} copy(bf16[256,4096]{1,0:T(8,128)(2,1)} %convolution_convert_fusion) | data formatting | bytes 4194304
  186.8 147.5 %reduce-scatter.4.cloned.1.call-done = bf16[128,256]{1,0:T(8,128)(2,1)} async-done(((bf16[4096,256]{1,0:T(8,128)(2,1)}), bf16[128,256]{1,0:T(8,128)(2,1)}) %reduce-scatter.4.cloned.1.call-update) | async-done | bytes 65552
  334.3 1.6 copy.10
  (22 shorter events, 0.1 us)
Async XLA Ops:
  6.5 79.9 %copy-start = (bf16[896,896]{1,0:T(8,128)(2,1)S(1)}, bf16[896,896]{1,0:T(8,128)(2,1)}, u32[]{:S(2)}) copy-start(bf16[896,896]{1,0:T(8,128)(2,1)} %param.13) | copy-start | bytes 4816900
  6.5 69.9 %all-gather.2.cloned.1.call-start = ((), (), s32[]{:S(2)}) async-start(), calls=%async_computation.1 | async-start | bytes 2162688 | tf_op jit(solution)/shard_map/all_gather | solution.py:33
  7.3 327.1 %reduce-scatter.4.cloned.1.call-start = ((), (), s32[]{:S(2)}) async-start(), calls=%async_computation.2 | async-start | bytes 2162688
  43.4 17.2 %copy-start.3 = (bf16[32,896]{1,0:T(8,128)(2,1)S(1)}, bf16[32,896]{1,0:T(8,128)(2,1)}, u32[]{:S(2)}) copy-start(bf16[32,896]{1,0:T(8,128)(2,1)} %param.10) | copy-start | bytes 172036
  43.4 17.2 %copy-start.4 = (bf16[32,896]{1,0:T(8,128)(2,1)S(1)}, bf16[32,896]{1,0:T(8,128)(2,1)}, u32[]{:S(2)}) copy-start(bf16[32,896]{1,0:T(8,128)(2,1)} %param.12) | copy-start | bytes 172036
  87.3 1.9 collective-permute-start
  89.3 12.6 %collective-permute-start.1 = (bf16[256,896]{1,0:T(8,128)(2,1)S(1)}, bf16[256,896]{1,0:T(8,128)(2,1)S(1)}, u32[]{:S(2)}, u32[]{:S(2)}) collective-permute-start(bf16[256,896]{1,0:T(8,128)(2,1)S(1)} %fusion.18), channel_id=1, source_target_pairs={{0,2},{1,3},{2,0},{3,1},{4,6},{5,7},{6,4},{7,5},{8,10},{9,11},{10,... | collective-permute-start | bytes 1376264 | tf_op jit(solution)/shard_map/ppermute | solution.py:12
  102.0 3.5 %copy-start.1 = (bf16[256,896]{1,0:T(8,128)(2,1)}, bf16[256,896]{1,0:T(8,128)(2,1)S(1)}, u32[]{:S(2)}) copy-start(bf16[256,896]{1,0:T(8,128)(2,1)S(1)} %collective-permute-done.1) | copy-start | bytes 1376260
  102.3 13.6 %collective-permute-start.2 = (bf16[256,896]{1,0:T(8,128)(2,1)S(1)}, bf16[256,896]{1,0:T(8,128)(2,1)}, u32[]{:S(2)}, u32[]{:S(2)}) collective-permute-start(bf16[256,896]{1,0:T(8,128)(2,1)S(1)} %fusion.26), channel_id=1, source_target_pairs={{0,4},{1,5},{2,6},{3,7},{4,0},{5,1},{6,2},{7,3},{8,12},{9,13},{10,... | collective-permute-start | bytes 1376264 | tf_op jit(solution)/shard_map/ppermute | solution.py:12
  118.3 11.1 %collective-permute-start.3 = (bf16[256,896]{1,0:T(8,128)(2,1)}, bf16[256,896]{1,0:T(8,128)(2,1)S(1)}, u32[]{:S(2)}, u32[]{:S(2)}) collective-permute-start(bf16[256,896]{1,0:T(8,128)(2,1)} %get-tuple-element.5), channel_id=1, source_target_pairs={{0,8},{1,9},{2,10},{3,11},{4,12},{5,13},{6,14},{7,15},{8,0},{9,1},... | collective-permute-start | bytes 1376264 | tf_op jit(solution)/shard_map/ppermute | solution.py:12
  130.3 45.4 %collective-permute-start.4 = (bf16[256,896]{1,0:T(8,128)(2,1)}, bf16[256,896]{1,0:T(8,128)(2,1)}, u32[]{:S(2)}, u32[]{:S(2)}) collective-permute-start(bf16[256,896]{1,0:T(8,128)(2,1)} %fusion.19), channel_id=1, source_target_pairs={{0,16},{1,17},{2,18},{3,19},{4,20},{5,21},{6,22},{7,23},{8,24},{9,... | collective-permute-start | bytes 1376264 | tf_op jit(solution)/shard_map/ppermute | solution.py:12
  147.1 17.1 %copy-start.2 = (bf16[7,4096]{1,0:T(8,128)(2,1)S(1)}, bf16[7,4096]{1,0:T(8,128)(2,1)}, u32[]{:S(2)}) copy-start(bf16[7,4096]{1,0:T(8,128)(2,1)} %param.15) | copy-start | bytes 172036
Sparse Core Ops, SparseCore 0:
  9.1 66.7 all-gather.1
  187.0 147.3 reduce-scatter.3
where the time goes:
time: 345 us; the launch traced here: 343 us
  waiting for transfers between devices  181 us (52%)
  local copies, waits for them, and re-layouts  80.8 us (23%)
  other arithmetic  39.8 us (12%)
  matrix products  17.8 us (5%)
  between operations  13.5 us (4%)
  starting transfers between devices  9.91 us (3%)
    unnamed x3, waiting for transfers between devices  148 us
    shift_right_arithmetic x10, local copies, waits for them, and re-layouts, unpack(): nibble = jnp.bitwise_and(jnp.right_shift(lifted[:, None, :], shifts), 15)  75.1 us
    ppermute x5, waiting for transfers between devices, from_partner(): return lax.ppermute(value, axis, pairs)  32.6 us
    convert_element_type x2, other arithmetic, unpack(): return values.reshape(row_count, col_count).astype(jnp.bfloat16)  27.2 us
    dot_general x1, matrix products, shards(): jnp.dot(lax.all_gather(tokens, 'tp', axis=1, tiled=True), w_both, preferr...  9.99 us
    ppermute x5, starting transfers between devices, from_partner(): return lax.ppermute(value, axis, pairs)  9.87 us
    add x3, other arithmetic, unpack(): lifted = packed + 32768  8.83 us
    dot_general x1, matrix products, shards(): partial_value = jnp.dot(rotated, w_down, preferred_element_type=jnp.float32)  7.05 us
  transfers between devices with their start and end apart: 7, of which 5 were waited for; matrix products, arithmetic and copies ran while one was open for 32% of the time, Pallas kernels for 0%

commit v1 on v0

v1 whole, which is shorter than its diff:
```python
import functools
import math

import jax
import jax.numpy as jnp
from jax import lax
from jax.experimental import pallas as pl
from jax.experimental.pallas import tpu as pltpu
from jax.sharding import PartitionSpec as P

MESH = pl.DeviceIdType.MESH
TP = 32
ROWS = 256
UNITS = 896
TILES = 7
CHUNKS = 2
CR = ROWS // CHUNKS
HALF = CR // 2
F32 = jnp.float32
BF16 = jnp.bfloat16


def field_order():
    source = lax.broadcasted_iota(jnp.int32, (128, 128), 0)
    target = lax.broadcasted_iota(jnp.int32, (128, 128), 1)
    return jnp.where(target == (source % 4) * 32 + source // 4, 1.0, 0.0).astype(BF16)


def decode(words, scale):
    flipped = jnp.bitwise_xor(words, 0x0888)
    planes = []
    for field in range(4):
        if field == 3:
            value = jnp.right_shift(words, 12)
        else:
            value = jnp.right_shift(jnp.left_shift(flipped, 28 - 4 * field), 28)
        scaled = value.astype(F32).reshape(4, 8, 128) * scale
        planes.append(scaled.reshape(32, 128).astype(BF16))
    return planes


def kernel(
    tok_in, gate_scales, up_scales, down_scales, gate_hbm, up_hbm, factor_hbm, down_hbm, out_ref,
    gate_codes, up_codes, down_codes, factor, tok, w_both, w_down, ordered, gate_f32, up_f32, down_f32,
    hidden, blocked, had_in, had_out, rotated, part, core_in, sums, first_in, second_in, mixed, z_in,
    load_sem, tok_send, tok_recv, a_send, a_recv, b_send, b_recv, c_send, c_recv, x_send, x_recv,
    y_send, y_recv, z_send, z_recv,
):
    me = lax.axis_index("tp")
    z, x, c = me // 8, (me // 2) % 4, me % 2
    other = me + 1 - 2 * c
    right = z * 8 + ((x + 1) % 4) * 2 + c
    left = z * 8 + ((x + 3) % 4) * 2 + c
    z_of = [z, z + 1 - 2 * (z % 2), (z + 2) % 4, 3 - z]

    barrier = pltpu.get_barrier_semaphore()

    @pl.loop(1, TP)
    def _(step):
        pl.semaphore_signal(barrier, inc=1, device_id={"tp": (me + step) % TP}, device_id_type=MESH)

    loads = []
    for piece in range(4):
        rows = pl.ds(256 * piece, 256)
        loads.append([
            pltpu.make_async_copy(gate_hbm.at[rows], gate_codes.at[rows], load_sem.at[piece]),
            pltpu.make_async_copy(up_hbm.at[rows], up_codes.at[rows], load_sem.at[4 + piece]),
        ])
        for copy in loads[-1]:
            copy.start()
    factor_load = pltpu.make_async_copy(factor_hbm, factor, load_sem.at[8])
    factor_load.start()
    down_load = pltpu.make_async_copy(down_hbm, down_codes, load_sem.at[9])
    down_load.start()

    order = field_order()

    def columns(block):
        return pl.ds(pl.multiple_of(block * 128, 128), 128)

    tok[:, columns(me)] = jnp.dot(tok_in[...], order, preferred_element_type=F32).astype(BF16)
    for source, spread, groups in ((gate_scales, gate_f32, 32), (up_scales, up_f32, 32), (down_scales, down_f32, 7)):
        scales = source[...].astype(F32)
        for group in range(groups):
            spread[group] = jnp.broadcast_to(scales[group : group + 1], spread.shape[1:])

    pl.semaphore_wait(barrier, TP - 1)

    waiting = []

    def pass_on(block, device, row=0, count=ROWS):
        where = tok.at[pl.ds(row, count), columns(block)]
        copy = pltpu.make_async_remote_copy(
            src_ref=where, dst_ref=where, send_sem=tok_send.at[len(waiting)],
            recv_sem=tok_recv.at[block, 1 if row else 0],
            device_id={"tp": device}, device_id_type=MESH,
        )
        copy.start()
        waiting.append(copy)

    def arrived(block, row=0, count=ROWS):
        where = tok.at[pl.ds(row, count), columns(block)]
        pltpu.make_async_copy(where, where, tok_recv.at[block, 1 if row else 0]).wait()

    def at(near, shift):
        return z_of[near] * 8 + ((x + shift) % 4) * 2 + c

    def from_z(near):
        if near:
            arrived(at(near, 0))
        else:
            for peer in (1, 2, 3):
                pass_on(me, at(peer, 0))
        pass_on(at(near, 0), right)
        pass_on(at(near, 0), left)
        pass_on(at(near, 0), other)

    def from_x(near):
        block = at(near, 3)
        arrived(block)
        pass_on(block, right, 0, ROWS // 2)
        pass_on(block, other)
        block = at(near, 1)
        arrived(block)
        pass_on(block, left, ROWS // 2, ROWS // 2)
        pass_on(block, other)

    def from_far(near):
        block = at(near, 2)
        arrived(block, 0, ROWS // 2)
        arrived(block, ROWS // 2, ROWS // 2)
        pass_on(block, other)

    def decode_piece(piece):
        for copy in loads[piece]:
            copy.wait()

        @pl.loop(8 * piece, 8 * piece + 8)
        def _(group):
            rows = pl.ds(pl.multiple_of(group * 32, 32), 32)
            for tile in range(TILES):
                cols = pl.ds(128 * tile, 128)
                for place, codes, scales in ((0, gate_codes, gate_f32), (128, up_codes, up_f32)):
                    planes = decode(codes[rows, cols], scales[group, :, cols])
                    for field, plane in enumerate(planes):
                        to = pl.ds(pl.multiple_of(group * 128 + 32 * field, 32), 32)
                        w_both[tile, to, pl.ds(place, 128)] = plane

    from_z(0)
    decode_piece(0)
    from_z(1)
    from_x(0)
    decode_piece(1)
    from_z(2)
    from_x(1)
    decode_piece(2)
    from_z(3)
    from_x(2)
    from_far(0)
    decode_piece(3)
    factor_load.wait()
    for tile in range(TILES):
        cols = pl.ds(128 * tile, 128)
        ordered[:, cols] = jnp.dot(factor[:, cols], order, preferred_element_type=F32).astype(BF16)
    from_x(3)
    from_far(1)
    from_far(2)
    from_far(3)

    @pl.loop(0, TP // 2)
    def _(chip):
        arrived(chip * 2 + 1 - c)

    @pl.loop(0, TILES)
    def _(tile):
        both = jnp.dot(tok[...], w_both[tile], preferred_element_type=F32)
        gate, up = both[:, :128], both[:, 128:]
        value = gate / (1.0 + jnp.exp(-gate)) * up
        hidden[:, pl.ds(pl.multiple_of(tile * 128, 128), 128)] = value.astype(BF16)

    def share(device):
        dz, dx, dc = device // 8, (device // 2) % 4, device % 2
        return dz * 2 + dx // 2, (dx % 2) * 2 + dc

    row_tile, quarter = share(me)
    wide = quarter < 3
    narrow = quarter == 3

    def two(start):
        return pl.ds(pl.multiple_of(start * 256, 256), 256)

    last = pl.ds(768, 128)

    def scatter(chunk):
        value = jnp.dot(hidden[pl.ds(chunk * CR, CR), :], ordered[...], preferred_element_type=F32)
        blocked[chunk] = value.astype(BF16).reshape(CR // 16, 16, UNITS)

        @pl.loop(1, TP)
        def _(step):
            device = (me + step) % TP
            tile, part_of = share(device)

            @pl.when(part_of < 3)
            def _():
                pltpu.make_async_remote_copy(
                    src_ref=blocked.at[chunk, tile, :, two(part_of)], dst_ref=had_in.at[chunk, me],
                    send_sem=a_send.at[chunk], recv_sem=a_recv.at[chunk],
                    device_id={"tp": device}, device_id_type=MESH,
                ).start()

            @pl.when(part_of == 3)
            def _():
                pltpu.make_async_remote_copy(
                    src_ref=blocked.at[chunk, tile, :, last], dst_ref=had_in.at[chunk, me, :, pl.ds(0, 128)],
                    send_sem=a_send.at[chunk], recv_sem=a_recv.at[chunk],
                    device_id={"tp": device}, device_id_type=MESH,
                ).start()

        @pl.when(wide)
        def _():
            pltpu.make_async_copy(
                blocked.at[chunk, row_tile, :, two(quarter)], had_in.at[chunk, me], a_recv.at[chunk]
            ).start()

        @pl.when(narrow)
        def _():
            pltpu.make_async_copy(
                blocked.at[chunk, row_tile, :, last], had_in.at[chunk, me, :, pl.ds(0, 128)], a_recv.at[chunk]
            ).start()

    def rotate(chunk):
        def combine(tile):
            cols = pl.ds(128 * tile, 128)
            held = [had_in[chunk, source, :, cols].astype(F32) for source in range(TP)]
            apart = 1
            while apart < TP:
                held = [
                    held[i - apart] - held[i] if i & apart else held[i] + held[i + apart]
                    for i in range(TP)
                ]
                apart *= 2
            for target in range(TP):
                had_out[chunk, target, :, cols] = (held[target] * (1.0 / math.sqrt(TP))).astype(BF16)

        def give(out_cols, to_cols):
            @pl.loop(1, TP)
            def _(step):
                device = (me + step) % TP
                pltpu.make_async_remote_copy(
                    src_ref=had_out.at[chunk, device, :, out_cols], dst_ref=rotated.at[chunk, row_tile, :, to_cols],
                    send_sem=b_send.at[chunk], recv_sem=b_recv.at[chunk],
                    device_id={"tp": device}, device_id_type=MESH,
                ).start()

            pltpu.make_async_copy(
                had_out.at[chunk, me, :, out_cols], rotated.at[chunk, row_tile, :, to_cols], b_recv.at[chunk]
            ).start()

        @pl.when(wide)
        def _():
            everything = had_in.at[chunk]
            pltpu.make_async_copy(everything, everything, a_recv.at[chunk]).wait()
            combine(0)
            combine(1)
            give(pl.ds(0, 256), two(quarter))

        @pl.when(narrow)
        def _():
            everything = had_in.at[chunk, :, :, pl.ds(0, 128)]
            pltpu.make_async_copy(everything, everything, a_recv.at[chunk]).wait()
            combine(0)
            give(pl.ds(0, 128), last)

    def remote(src, dst, send, recv, device):
        copy = pltpu.make_async_remote_copy(
            src_ref=src, dst_ref=dst, send_sem=send, recv_sem=recv,
            device_id={"tp": device}, device_id_type=MESH,
        )
        copy.start()
        waiting.append(copy)
        return copy

    x_of = [x, (x + 1) % 4, (x + 2) % 4, (x + 3) % 4]
    from_core = {}

    def down(chunk):
        everything = rotated.at[chunk]
        pltpu.make_async_copy(everything, everything, b_recv.at[chunk]).wait()
        for shift in (2, 1, 3, 0):
            place = x_of[shift]

            @pl.loop(0, 4)
            def _(z_to):
                both = jnp.dot(
                    rotated[chunk].reshape(CR, UNITS), w_down[z_to * 4 + place], preferred_element_type=F32
                ).astype(BF16)
                part[chunk, 0, place, z_to] = both[:, :128]
                part[chunk, 1, place, z_to] = both[:, 128:]

            from_core[chunk, shift] = remote(
                part.at[chunk, 1 - c, place], core_in.at[chunk, shift],
                c_send.at[chunk, shift], c_recv.at[chunk, shift], other,
            )

    top, bottom = pl.ds(0, HALF), pl.ds(HALF, HALF)

    def join(chunk, shift, rows):
        return part[chunk, c, x_of[shift], :, rows].astype(F32) + core_in[chunk, shift, :, rows].astype(F32)

    x_copies = {}

    def x_first(chunk):
        from_core[chunk, 2].wait_recv()
        sums[chunk, 2] = join(chunk, 2, pl.ds(0, CR)).astype(BF16)
        x_copies[chunk, "r1"] = remote(
            sums.at[chunk, 2, :, top], first_in.at[chunk, 0], x_send.at[chunk, 0], x_recv.at[chunk, 0], right
        )
        x_copies[chunk, "l1"] = remote(
            sums.at[chunk, 2, :, bottom], first_in.at[chunk, 1], x_send.at[chunk, 1], x_recv.at[chunk, 1], left
        )
        from_core[chunk, 1].wait_recv()
        sums[chunk, 1, :, bottom] = join(chunk, 1, bottom).astype(BF16)
        from_core[chunk, 3].wait_recv()
        sums[chunk, 3, :, top] = join(chunk, 3, top).astype(BF16)

    def x_second(chunk):
        x_copies[chunk, "r1"].wait_recv()
        sums[chunk, 1, :, top] = (join(chunk, 1, top) + first_in[chunk, 0].astype(F32)).astype(BF16)
        x_copies[chunk, "r2"] = remote(
            sums.at[chunk, 1], second_in.at[chunk, 0], y_send.at[chunk, 0], y_recv.at[chunk, 0], right
        )
        x_copies[chunk, "l1"].wait_recv()
        sums[chunk, 3, :, bottom] = (join(chunk, 3, bottom) + first_in[chunk, 1].astype(F32)).astype(BF16)
        x_copies[chunk, "l2"] = remote(
            sums.at[chunk, 3], second_in.at[chunk, 1], y_send.at[chunk, 1], y_recv.at[chunk, 1], left
        )
        from_core[chunk, 0].wait_recv()

    z_copies = {}

    def z_first(chunk):
        x_copies[chunk, "r2"].wait_recv()
        x_copies[chunk, "l2"].wait_recv()
        for near in (3, 2, 1, 0):
            to = z_of[near]
            value = (
                part[chunk, c, x, to].astype(F32) + core_in[chunk, 0, to].astype(F32)
                + second_in[chunk, 0, to].astype(F32) + second_in[chunk, 1, to].astype(F32)
            )
            mixed[chunk, near] = value.astype(BF16)
            if near:
                z_copies[chunk, near] = remote(
                    mixed.at[chunk, near], z_in.at[chunk, near], z_send.at[chunk, near], z_recv.at[chunk, near],
                    to * 8 + x * 2 + c,
                )

    def z_last(chunk):
        total = mixed[chunk, 0].astype(F32)
        for near in (1, 2, 3):
            z_copies[chunk, near].wait_recv()
            total = total + z_in[chunk, near].astype(F32)
        out_ref[pl.ds(chunk * CR, CR), :] = total.astype(BF16)

    scatter(0)
    scatter(1)

    down_load.wait()

    @pl.loop(0, 16)
    def _(chip):
        for group in range(TILES):
            for side in range(2):
                cols = pl.ds(pl.multiple_of(chip * 256 + 128 * side, 128), 128)
                planes = decode(down_codes[pl.ds(32 * group, 32), cols], down_f32[group, :, cols])
                for field, plane in enumerate(planes):
                    w_down[chip, pl.ds(128 * group + 32 * field, 32), pl.ds(128 * side, 128)] = plane

    rotate(0)
    rotate(1)
    down(0)
    x_first(0)
    down(1)
    x_second(0)
    x_first(1)
    z_first(0)
    x_second(1)
    z_last(0)
    z_first(1)
    z_last(1)

    for copy in waiting:
        copy.wait_send()
    for chunk in range(CHUNKS):
        for mine, tiles_sent, slot in ((wide, 54, 256), (narrow, 55, 128)):
            @pl.when(mine)
            def _():
                sent = w_both.at[0, pl.ds(0, 16 * tiles_sent), pl.ds(0, 128)]
                pltpu.make_async_copy(sent, sent, a_send.at[chunk]).wait()
                sent = had_out.at[chunk, pl.ds(0, TP - 1), :, pl.ds(0, slot)]
                pltpu.make_async_copy(sent, sent, b_send.at[chunk]).wait()


def shards(tokens, gate_codes, gate_scales, up_codes, up_scales, local_factor, down_codes, down_scales):
    vmem, hbm, dma = pl.BlockSpec(memory_space=pltpu.VMEM), pl.BlockSpec(memory_space=pl.ANY), pltpu.SemaphoreType.DMA
    return pl.pallas_call(
        kernel,
        out_shape=jax.ShapeDtypeStruct((ROWS, 128), BF16),
        in_specs=[vmem] * 4 + [hbm] * 4,
        out_specs=vmem,
        scratch_shapes=[
            pltpu.VMEM((1024, UNITS), jnp.int32),
            pltpu.VMEM((1024, UNITS), jnp.int32),
            pltpu.VMEM((224, 4096), jnp.int32),
            pltpu.VMEM((UNITS, UNITS), BF16),
            pltpu.VMEM((ROWS, 4096), BF16),
            pltpu.VMEM((TILES, 4096, 256), BF16),
            pltpu.VMEM((16, UNITS, 256), BF16),
            pltpu.VMEM((UNITS, UNITS), BF16),
            pltpu.VMEM((32, 8, UNITS), F32),
            pltpu.VMEM((32, 8, UNITS), F32),
            pltpu.VMEM((7, 8, 4096), F32),
            pltpu.VMEM((ROWS, UNITS), BF16),
            pltpu.VMEM((CHUNKS, CR // 16, 16, UNITS), BF16),
            pltpu.VMEM((CHUNKS, TP, 16, 256), BF16),
            pltpu.VMEM((CHUNKS, TP, 16, 256), BF16),
            pltpu.VMEM((CHUNKS, CR // 16, 16, UNITS), BF16),
            pltpu.VMEM((CHUNKS, 2, 4, 4, CR, 128), BF16),
            pltpu.VMEM((CHUNKS, 4, 4, CR, 128), BF16),
            pltpu.VMEM((CHUNKS, 4, 4, CR, 128), BF16),
            pltpu.VMEM((CHUNKS, 2, 4, HALF, 128), BF16),
            pltpu.VMEM((CHUNKS, 2, 4, CR, 128), BF16),
            pltpu.VMEM((CHUNKS, 4, CR, 128), BF16),
            pltpu.VMEM((CHUNKS, 4, CR, 128), BF16),
            dma((10,)),
            dma((48,)),
            dma((TP, 2)),
            dma((CHUNKS,)),
            dma((CHUNKS,)),
            dma((CHUNKS,)),
            dma((CHUNKS,)),
            dma((CHUNKS, 4)),
            dma((CHUNKS, 4)),
            dma((CHUNKS, 2)),
            dma((CHUNKS, 2)),
            dma((CHUNKS, 2)),
            dma((CHUNKS, 2)),
            dma((CHUNKS, 4)),
            dma((CHUNKS, 4)),
        ],
        compiler_params=pltpu.CompilerParams(
            collective_id=0, has_side_effects=True, vmem_limit_bytes=58 * 1024 * 1024
        ),
        name="feed_forward",
    )(tokens, gate_scales, up_scales, down_scales, gate_codes, up_codes, local_factor, down_codes)


def solution(mesh):
    return jax.shard_map(
        shards,
        mesh=mesh,
        in_specs=(
            P("req", "tp"),
            P(None, "tp"),
            P(None, "tp"),
            P(None, "tp"),
            P(None, "tp"),
            P(),
            P("tp", None),
            P("tp", None),
        ),
        out_specs=P("req", "tp"),
        check_vma=False,
    )
```

time: 345 us -> 78.6 us (0.23)
  waiting for transfers between devices: 181 us -> 0 us
  local copies, waits for them, and re-layouts: 80.8 us -> 1.47 us
  Pallas kernels: 0 us -> 76.9 us
  other arithmetic: 39.8 us -> 0 us
  matrix products: 17.8 us -> 0 us
  between operations: 13.5 us -> 0.01 us
  starting transfers between devices: 9.91 us -> 0 us
    unnamed x3 -> x0, waiting for transfers between devices: 148 us -> none
    pallas_call x0 -> x1, Pallas kernels: none -> 76.9 us  [shards(): pl.pallas_call(kernel, out_shape=jax.ShapeDtypeStruct((ROWS, 128), BF16),...]
    shift_right_arithmetic x10 -> x0, local copies, waits for them, and re-layouts: 75.1 us -> none  [unpack(): nibble = jnp.bitwise_and(jnp.right_shift(lifted[:, None, :], shifts), 15)]
    ppermute x5 -> x0, waiting for transfers between devices: 32.6 us -> none  [from_partner(): return lax.ppermute(value, axis, pairs)]
    convert_element_type x9 -> x0, other arithmetic: 31 us -> none  [the longest x2 27.2 us: unpack(): return values.reshape(row_count, col_count).astype(jnp.bfloat16)]
    dot_general x3 -> x0, matrix products: 17.8 us -> none  [the longest x1 9.99 us: shards(): jnp.dot(lax.all_gather(tokens, 'tp', axis=1, tiled=True), w_both, preferr...]
    ppermute x5 -> x0, starting transfers between devices: 9.87 us -> none  [from_partner(): return lax.ppermute(value, axis, pairs)]
    add x3 -> x0, other arithmetic: 8.83 us -> none  [unpack(): lifted = packed + 32768]
  transfers between devices with their start and end apart: 7 -> 0, of which waited for: 5 -> 0; matrix products, arithmetic and copies ran while one was open for 32% -> 0% of each run, Pallas kernels for 0% -> 0%
where the time goes in v1:
time: 78.6 us; the launch traced here: 78.4 us
  Pallas kernels  76.9 us (98%)
  local copies, waits for them, and re-layouts  1.47 us (2%)
    pallas_call x1, Pallas kernels, shards(): pl.pallas_call(kernel, out_shape=jax.ShapeDtypeStruct((ROWS, 128), BF16),...  76.9 us

profile of v1, /device:TPU:16, one launch (start us, length us, event | category | flops | bytes accessed | tf_op | source)
XLA Modules:
  0.0 78.4 jit_solution(14245829381629485882)
XLA Ops:
  0.0 76.9 %feed_forward.1 = bf16[256,128]{1,0:T(8,128)(2,1)} custom-call(bf16[256,128]{1,0:T(8,128)(2,1)} %tok_in.1, bf16[32,896]{1,0:T(8,128)(2,1)} %gate_scales.1, bf16[32,896]{1,0:T(8,128)(2,1)} %up_scales.1, bf16[7,4096]{1,0:T(8,128)(2,1)} %down_scales.1, s32[1024,896]{1,0:T(8,128)} %gate_hbm.1, s32[1024,896]{1,0:T(8,128)} %up_hbm.1, bf16[896,896]{1,0:T(8,128)(2,1)} %factor_hbm.1, ...), custom_call_target="tpu_custom_call" | custom-call | tf_op jit(solution)/shard_map/feed_forward/pallas_call | solution.py:405
  76.9 1.5 %copy.10 = bf16[256,128]{1,0:T(8,128)(2,1)} copy(bf16[256,128]{1,0:T(8,128)(2,1)} %feed_forward.1) | data formatting | bytes 131072

commit v2 on v1

--- a/solution.py
+++ b/solution.py
@@ -41,23 +41,56 @@
 
 def kernel(
     tok_in, gate_scales, up_scales, down_scales, gate_hbm, up_hbm, factor_hbm, down_hbm, out_ref,
-    gate_codes, up_codes, down_codes, factor, tok, w_both, w_down, ordered, gate_f32, up_f32, down_f32,
+    staged, gate_codes, up_codes, down_codes, factor, tok, w_both, w_down, ordered, gate_f32, up_f32, down_f32,
     hidden, blocked, had_in, had_out, rotated, part, core_in, sums, first_in, second_in, mixed, z_in,
     load_sem, tok_send, tok_recv, a_send, a_recv, b_send, b_recv, c_send, c_recv, x_send, x_recv,
     y_send, y_recv, z_send, z_recv,
 ):
-    me = lax.axis_index("tp")
+    me, mine = lax.axis_index("tp"), lax.axis_index("req")
     z, x, c = me // 8, (me // 2) % 4, me % 2
+    upper, plane = mine % 2, mine - mine % 2
+    low = z < 2
     other = me + 1 - 2 * c
     right = z * 8 + ((x + 1) % 4) * 2 + c
     left = z * 8 + ((x + 3) % 4) * 2 + c
     z_of = [z, z + 1 - 2 * (z % 2), (z + 2) % 4, 3 - z]
 
+    served = jnp.where(low, 1 - upper, upper)
+
+    def window(request, device_z):
+        return plane + jnp.where(device_z < 2, 1 - request, request)
+
+    def member(chunk, device):
+        return {"req": window(served, device // 8) if chunk else mine, "tp": device}
+
+    def worker(chunk, device):
+        return {"req": window(upper, device // 8) if chunk else mine, "tp": device}
+
+    def owner(chunk, device):
+        return {"req": plane + served if chunk else mine, "tp": device}
+
+    def here(device):
+        return {"req": mine, "tp": device}
+
     barrier = pltpu.get_barrier_semaphore()
+
+    def greet(device):
+        pl.semaphore_signal(barrier, inc=1, device_id=device, device_id_type=MESH)
 
     @pl.loop(1, TP)
     def _(step):
-        pl.semaphore_signal(barrier, inc=1, device_id={"tp": (me + step) % TP}, device_id_type=MESH)
+        greet(here((me + step) % TP))
+
+    far_side = jnp.where(low, 16, 0)
+
+    @pl.loop(0, 16)
+    def _(step):
+        greet({"req": plane + 1 - upper, "tp": far_side + step})
+
+    @pl.when(low)
+    def _():
+        for near in range(2):
+            greet({"req": plane + 1 - upper, "tp": near * 8 + x * 2 + c})
 
     loads = []
     for piece in range(4):
@@ -78,105 +111,123 @@
     def columns(block):
         return pl.ds(pl.multiple_of(block * 128, 128), 128)
 
-    tok[:, columns(me)] = jnp.dot(tok_in[...], order, preferred_element_type=F32).astype(BF16)
+    staged[...] = jnp.dot(tok_in[...], order, preferred_element_type=F32).astype(BF16)
+    tok[pl.ds(0, CR), columns(me)] = staged[pl.ds(0, CR), :]
+
+    @pl.when(jnp.logical_not(low))
+    def _():
+        tok[pl.ds(CR, CR), columns(me)] = staged[pl.ds(CR, CR), :]
+
     for source, spread, groups in ((gate_scales, gate_f32, 32), (up_scales, up_f32, 32), (down_scales, down_f32, 7)):
         scales = source[...].astype(F32)
         for group in range(groups):
             spread[group] = jnp.broadcast_to(scales[group : group + 1], spread.shape[1:])
 
-    pl.semaphore_wait(barrier, TP - 1)
+    pl.semaphore_wait(barrier, TP + 15 + jnp.where(low, 2, 0))
 
     waiting = []
 
-    def pass_on(block, device, row=0, count=ROWS):
-        where = tok.at[pl.ds(row, count), columns(block)]
+    def remote(src, dst, send, recv, device):
         copy = pltpu.make_async_remote_copy(
-            src_ref=where, dst_ref=where, send_sem=tok_send.at[len(waiting)],
-            recv_sem=tok_recv.at[block, 1 if row else 0],
-            device_id={"tp": device}, device_id_type=MESH,
+            src_ref=src, dst_ref=dst, send_sem=send, recv_sem=recv, device_id=device, device_id_type=MESH,
         )
         copy.start()
         waiting.append(copy)
-
-    def arrived(block, row=0, count=ROWS):
-        where = tok.at[pl.ds(row, count), columns(block)]
-        pltpu.make_async_copy(where, where, tok_recv.at[block, 1 if row else 0]).wait()
+        return copy
+
+    def rows_of(chunk, part):
+        if part is None:
+            return pl.ds(chunk * CR, CR)
+        return pl.ds(chunk * CR + part * HALF, HALF)
+
+    def slot(chunk, block, part):
+        return tok_recv.at[chunk, block, part or 0]
+
+    def pass_on(chunk, block, device, part=None):
+        where = tok.at[rows_of(chunk, part), columns(block)]
+        remote(where, where, tok_send.at[len(waiting)], slot(chunk, block, part), here(device))
+
+    def arrived(chunk, block, part=None):
+        where = tok.at[rows_of(chunk, part), columns(block)]
+        pltpu.make_async_copy(where, where, slot(chunk, block, part)).wait()
 
     def at(near, shift):
         return z_of[near] * 8 + ((x + shift) % 4) * 2 + c
 
-    def from_z(near):
+    def send_own(chunk):
+        for near in (3, 2, 1):
+            remote(
+                staged.at[rows_of(chunk, None)], tok.at[rows_of(chunk, None), columns(me)],
+                tok_send.at[len(waiting)], slot(chunk, me, None), worker(chunk, at(near, 0)),
+            )
+        if chunk:
+            @pl.when(low)
+            def _():
+                own_copy().start()
+
+    def own_copy():
+        return pltpu.make_async_remote_copy(
+            src_ref=staged.at[rows_of(1, None)], dst_ref=tok.at[rows_of(1, None), columns(me)],
+            send_sem=tok_send.at[95], recv_sem=slot(1, me, None), device_id=worker(1, me), device_id_type=MESH,
+        )
+
+    def from_z(chunk, near):
+        block = at(near, 0)
         if near:
-            arrived(at(near, 0))
-        else:
-            for peer in (1, 2, 3):
-                pass_on(me, at(peer, 0))
-        pass_on(at(near, 0), right)
-        pass_on(at(near, 0), left)
-        pass_on(at(near, 0), other)
-
-    def from_x(near):
+            arrived(chunk, block)
+        elif chunk:
+            @pl.when(low)
+            def _():
+                arrived(chunk, block)
+        pass_on(chunk, block, right)
+        pass_on(chunk, block, left)
+        pass_on(chunk, block, other)
+
+    def from_x(chunk, near):
         block = at(near, 3)
-        arrived(block)
-        pass_on(block, right, 0, ROWS // 2)
-        pass_on(block, other)
+        arrived(chunk, block)
+        pass_on(chunk, block, right, 0)
+        pass_on(chunk, block, other)
         block = at(near, 1)
-        arrived(block)
-        pass_on(block, left, ROWS // 2, ROWS // 2)
-        pass_on(block, other)
-
-    def from_far(near):
+        arrived(chunk, block)
+        pass_on(chunk, block, left, 1)
+        pass_on(chunk, block, other)
+
+    def from_far(chunk, near):
         block = at(near, 2)
-        arrived(block, 0, ROWS // 2)
-        arrived(block, ROWS // 2, ROWS // 2)
-        pass_on(block, other)
+        arrived(chunk, block, 0)
+        arrived(chunk, block, 1)
+        pass_on(chunk, block, other)
+
+    def from_core(chunk):
+        @pl.loop(0, TP // 2)
+        def _(chip):
+            arrived(chunk, chip * 2 + 1 - c)
 
     def decode_piece(piece):
-        for copy in loads[piece]:
-            copy.wait()
-
-        @pl.loop(8 * piece, 8 * piece + 8)
+        if piece % 2 == 0:
+            for copy in loads[piece // 2]:
+                copy.wait()
+
+        @pl.loop(4 * piece, 4 * piece + 4)
         def _(group):
             rows = pl.ds(pl.multiple_of(group * 32, 32), 32)
             for tile in range(TILES):
                 cols = pl.ds(128 * tile, 128)
                 for place, codes, scales in ((0, gate_codes, gate_f32), (128, up_codes, up_f32)):
                     planes = decode(codes[rows, cols], scales[group, :, cols])
-                    for field, plane in enumerate(planes):
+                    for field, plane_of in enumerate(planes):
                         to = pl.ds(pl.multiple_of(group * 128 + 32 * field, 32), 32)
-                        w_both[tile, to, pl.ds(place, 128)] = plane
-
-    from_z(0)
-    decode_piece(0)
-    from_z(1)
-    from_x(0)
-    decode_piece(1)
-    from_z(2)
-    from_x(1)
-    decode_piece(2)
-    from_z(3)
-    from_x(2)
-    from_far(0)
-    decode_piece(3)
-    factor_load.wait()
-    for tile in range(TILES):
-        cols = pl.ds(128 * tile, 128)
-        ordered[:, cols] = jnp.dot(factor[:, cols], order, preferred_element_type=F32).astype(BF16)
-    from_x(3)
-    from_far(1)
-    from_far(2)
-    from_far(3)
-
-    @pl.loop(0, TP // 2)
-    def _(chip):
-        arrived(chip * 2 + 1 - c)
-
-    @pl.loop(0, TILES)
-    def _(tile):
-        both = jnp.dot(tok[...], w_both[tile], preferred_element_type=F32)
-        gate, up = both[:, :128], both[:, 128:]
-        value = gate / (1.0 + jnp.exp(-gate)) * up
-        hidden[:, pl.ds(pl.multiple_of(tile * 128, 128), 128)] = value.astype(BF16)
+                        w_both[tile, to, pl.ds(place, 128)] = plane_of
+
+    def gate_up(chunk, first, stop):
+        @pl.loop(first, stop)
+        def _(tile):
+            rows = rows_of(chunk, None)
+            both = jnp.dot(tok[rows, :], w_both[tile], preferred_element_type=F32)
+            gate, up = both[:, :128], both[:, 128:]
+            value = gate / (1.0 + jnp.exp(-gate)) * up
+            hidden[rows, pl.ds(pl.multiple_of(tile * 128, 128), 128)] = value.astype(BF16)
 
     def share(device):
         dz, dx, dc = device // 8, (device // 2) % 4, device % 2
@@ -197,7 +248,7 @@
 
         @pl.loop(1, TP)
         def _(step):
-            device = (me + step) % TP
+            device = (me + 1 + (step + 6) % (TP - 1)) % TP
             tile, part_of = share(device)
 
             @pl.when(part_of < 3)
@@ -205,7 +256,7 @@
                 pltpu.make_async_remote_copy(
                     src_ref=blocked.at[chunk, tile, :, two(part_of)], dst_ref=had_in.at[chunk, me],
                     send_sem=a_send.at[chunk], recv_sem=a_recv.at[chunk],
-                    device_id={"tp": device}, device_id_type=MESH,
+                    device_id=member(chunk, device), device_id_type=MESH,
                 ).start()
 
             @pl.when(part_of == 3)
@@ -213,7 +264,7 @@
                 pltpu.make_async_remote_copy(
                     src_ref=blocked.at[chunk, tile, :, last], dst_ref=had_in.at[chunk, me, :, pl.ds(0, 128)],
                     send_sem=a_send.at[chunk], recv_sem=a_recv.at[chunk],
-                    device_id={"tp": device}, device_id_type=MESH,
+                    device_id=member(chunk, device), device_id_type=MESH,
                 ).start()
 
         @pl.when(wide)
@@ -245,11 +296,11 @@
         def give(out_cols, to_cols):
             @pl.loop(1, TP)
             def _(step):
-                device = (me + step) % TP
+                device = (me + 1 + (step + 6) % (TP - 1)) % TP
                 pltpu.make_async_remote_copy(
                     src_ref=had_out.at[chunk, device, :, out_cols], dst_ref=rotated.at[chunk, row_tile, :, to_cols],
                     send_sem=b_send.at[chunk], recv_sem=b_recv.at[chunk],
-                    device_id={"tp": device}, device_id_type=MESH,
+                    device_id=member(chunk, device), device_id_type=MESH,
                 ).start()
 
             pltpu.make_async_copy(
@@ -271,17 +322,8 @@
             combine(0)
             give(pl.ds(0, 128), last)
 
-    def remote(src, dst, send, recv, device):
-        copy = pltpu.make_async_remote_copy(
-            src_ref=src, dst_ref=dst, send_sem=send, recv_sem=recv,
-            device_id={"tp": device}, device_id_type=MESH,
-        )
-        copy.start()
-        waiting.append(copy)
-        return copy
-
     x_of = [x, (x + 1) % 4, (x + 2) % 4, (x + 3) % 4]
-    from_core = {}
+    from_other = {}
 
     def down(chunk):
         everything = rotated.at[chunk]
@@ -297,9 +339,9 @@
                 part[chunk, 0, place, z_to] = both[:, :128]
                 part[chunk, 1, place, z_to] = both[:, 128:]
 
-            from_core[chunk, shift] = remote(
+            from_other[chunk, shift] = remote(
                 part.at[chunk, 1 - c, place], core_in.at[chunk, shift],
-                c_send.at[chunk, shift], c_recv.at[chunk, shift], other,
+                c_send.at[chunk, shift], c_recv.at[chunk, shift], here(other),
             )
 
     top, bottom = pl.ds(0, HALF), pl.ds(HALF, HALF)
@@ -310,31 +352,31 @@
     x_copies = {}
 
     def x_first(chunk):
-        from_core[chunk, 2].wait_recv()
+        from_other[chunk, 2].wait_recv()
         sums[chunk, 2] = join(chunk, 2, pl.ds(0, CR)).astype(BF16)
         x_copies[chunk, "r1"] = remote(
-            sums.at[chunk, 2, :, top], first_in.at[chunk, 0], x_send.at[chunk, 0], x_recv.at[chunk, 0], right
+            sums.at[chunk, 2, :, top], first_in.at[chunk, 0], x_send.at[chunk, 0], x_recv.at[chunk, 0], here(right)
         )
         x_copies[chunk, "l1"] = remote(
-            sums.at[chunk, 2, :, bottom], first_in.at[chunk, 1], x_send.at[chunk, 1], x_recv.at[chunk, 1], left
-        )
-        from_core[chunk, 1].wait_recv()
+            sums.at[chunk, 2, :, bottom], first_in.at[chunk, 1], x_send.at[chunk, 1], x_recv.at[chunk, 1], here(left)
+        )
+        from_other[chunk, 1].wait_recv()
         sums[chunk, 1, :, bottom] = join(chunk, 1, bottom).astype(BF16)
-        from_core[chunk, 3].wait_recv()
+        from_other[chunk, 3].wait_recv()
         sums[chunk, 3, :, top] = join(chunk, 3, top).astype(BF16)
 
     def x_second(chunk):
         x_copies[chunk, "r1"].wait_recv()
         sums[chunk, 1, :, top] = (join(chunk, 1, top) + first_in[chunk, 0].astype(F32)).astype(BF16)
         x_copies[chunk, "r2"] = remote(
-            sums.at[chunk, 1], second_in.at[chunk, 0], y_send.at[chunk, 0], y_recv.at[chunk, 0], right
+            sums.at[chunk, 1], second_in.at[chunk, 0], y_send.at[chunk, 0], y_recv.at[chunk, 0], here(right)
         )
         x_copies[chunk, "l1"].wait_recv()
         sums[chunk, 3, :, bottom] = (join(chunk, 3, bottom) + first_in[chunk, 1].astype(F32)).astype(BF16)
         x_copies[chunk, "l2"] = remote(
-            sums.at[chunk, 3], second_in.at[chunk, 1], y_send.at[chunk, 1], y_recv.at[chunk, 1], left
-        )
-        from_core[chunk, 0].wait_recv()
+            sums.at[chunk, 3], second_in.at[chunk, 1], y_send.at[chunk, 1], y_recv.at[chunk, 1], here(left)
+        )
+        from_other[chunk, 0].wait_recv()
 
     z_copies = {}
 
@@ -351,17 +393,86 @@
             if near:
                 z_copies[chunk, near] = remote(
                     mixed.at[chunk, near], z_in.at[chunk, near], z_send.at[chunk, near], z_recv.at[chunk, near],
-                    to * 8 + x * 2 + c,
+                    owner(chunk, to * 8 + x * 2 + c),
                 )
+        if chunk:
+            @pl.when(low)
+            def _():
+                own_sum().start()
+
+    def own_sum():
+        return pltpu.make_async_remote_copy(
+            src_ref=mixed.at[1, 0], dst_ref=z_in.at[1, 0], send_sem=z_send.at[1, 0], recv_sem=z_recv.at[1, 0],
+            device_id=owner(1, me), device_id_type=MESH,
+        )
 
     def z_last(chunk):
-        total = mixed[chunk, 0].astype(F32)
         for near in (1, 2, 3):
             z_copies[chunk, near].wait_recv()
-            total = total + z_in[chunk, near].astype(F32)
-        out_ref[pl.ds(chunk * CR, CR), :] = total.astype(BF16)
-
+
+        def finish(total):
+            for near in (1, 2, 3):
+                total = total + z_in[chunk, near].astype(F32)
+            out_ref[pl.ds(chunk * CR, CR), :] = total.astype(BF16)
+
+        if chunk:
+            @pl.when(low)
+            def _():
+                own_sum().wait_recv()
+                finish(z_in[chunk, 0].astype(F32))
+
+            @pl.when(jnp.logical_not(low))
+            def _():
+                finish(mixed[chunk, 0].astype(F32))
+        else:
+            finish(mixed[chunk, 0].astype(F32))
+
+    send_own(0)
+    from_z(0, 0)
+    decode_piece(0)
+    decode_piece(1)
+    from_z(0, 1)
+    from_x(0, 0)
+    decode_piece(2)
+    from_z(0, 2)
+    from_x(0, 1)
+    decode_piece(3)
+    from_z(0, 3)
+    from_x(0, 2)
+    from_far(0, 0)
+    send_own(1)
+    decode_piece(4)
+    from_x(0, 3)
+    from_far(0, 1)
+    decode_piece(5)
+    from_far(0, 2)
+    from_far(0, 3)
+    decode_piece(6)
+    from_z(1, 1)
+    from_z(1, 2)
+    decode_piece(7)
+    factor_load.wait()
+    for tile in range(TILES):
+        cols = pl.ds(128 * tile, 128)
+        ordered[:, cols] = jnp.dot(factor[:, cols], order, preferred_element_type=F32).astype(BF16)
+    from_z(1, 3)
+    from_z(1, 0)
+    from_x(1, 1)
+    from_core(0)
+    gate_up(0, 0, 2)
+    from_x(1, 2)
+    from_x(1, 3)
+    gate_up(0, 2, 4)
+    from_x(1, 0)
+    from_far(1, 1)
+    gate_up(0, 4, 6)
+    from_far(1, 2)
+    from_far(1, 3)
+    gate_up(0, 6, 7)
     scatter(0)
+    from_far(1, 0)
+    from_core(1)
+    gate_up(1, 0, 7)
     scatter(1)
 
     down_load.wait()
@@ -372,8 +483,8 @@
             for side in range(2):
                 cols = pl.ds(pl.multiple_of(chip * 256 + 128 * side, 128), 128)
                 planes = decode(down_codes[pl.ds(32 * group, 32), cols], down_f32[group, :, cols])
-                for field, plane in enumerate(planes):
-                    w_down[chip, pl.ds(128 * group + 32 * field, 32), pl.ds(128 * side, 128)] = plane
+                for field, plane_of in enumerate(planes):
+                    w_down[chip, pl.ds(128 * group + 32 * field, 32), pl.ds(128 * side, 128)] = plane_of
 
     rotate(0)
     rotate(1)
@@ -388,15 +499,20 @@
     z_first(1)
     z_last(1)
 
+    @pl.when(low)
+    def _():
+        own_copy().wait_send()
+        own_sum().wait_send()
+
     for copy in waiting:
         copy.wait_send()
     for chunk in range(CHUNKS):
-        for mine, tiles_sent, slot in ((wide, 54, 256), (narrow, 55, 128)):
-            @pl.when(mine)
+        for kind, tiles_sent, width in ((wide, 54, 256), (narrow, 55, 128)):
+            @pl.when(kind)
             def _():
                 sent = w_both.at[0, pl.ds(0, 16 * tiles_sent), pl.ds(0, 128)]
                 pltpu.make_async_copy(sent, sent, a_send.at[chunk]).wait()
-                sent = had_out.at[chunk, pl.ds(0, TP - 1), :, pl.ds(0, slot)]
+                sent = had_out.at[chunk, pl.ds(0, TP - 1), :, pl.ds(0, width)]
                 pltpu.make_async_copy(sent, sent, b_send.at[chunk]).wait()
 
 
@@ -408,6 +524,7 @@
         in_specs=[vmem] * 4 + [hbm] * 4,
         out_specs=vmem,
         scratch_shapes=[
+            pltpu.VMEM((ROWS, 128), BF16),
             pltpu.VMEM((1024, UNITS), jnp.int32),
             pltpu.VMEM((1024, UNITS), jnp.int32),
             pltpu.VMEM((224, 4096), jnp.int32),
@@ -432,8 +549,8 @@
             pltpu.VMEM((CHUNKS, 4, CR, 128), BF16),
             pltpu.VMEM((CHUNKS, 4, CR, 128), BF16),
             dma((10,)),
-            dma((48,)),
-            dma((TP, 2)),
+            dma((96,)),
+            dma((CHUNKS, TP, 2)),
             dma((CHUNKS,)),
             dma((CHUNKS,)),
             dma((CHUNKS,)),

time: 78.6 us -> 84.2 us (1.071)
  Pallas kernels: 76.9 us -> 81.9 us
    pallas_call x1, Pallas kernels: 76.9 us -> 81.9 us  [shards(): pl.pallas_call(kernel, out_shape=jax.ShapeDtypeStruct((ROWS, 128), BF16),...]
where the time goes in v2:
time: 84.2 us; the launch traced here: 83.3 us
  Pallas kernels  81.9 us (97%)
  local copies, waits for them, and re-layouts  1.47 us (2%)
    pallas_call x1, Pallas kernels, shards(): pl.pallas_call(kernel, out_shape=jax.ShapeDtypeStruct((ROWS, 128), BF16),...  81.9 us

profile of v2, /device:TPU:16, one launch (start us, length us, event | category | flops | bytes accessed | tf_op | source)
XLA Modules:
  0.0 83.3 jit_solution(4274643454605582982)
XLA Ops:
  0.0 81.9 %feed_forward.1 = bf16[256,128]{1,0:T(8,128)(2,1)} custom-call(bf16[256,128]{1,0:T(8,128)(2,1)} %tok_in.1, bf16[32,896]{1,0:T(8,128)(2,1)} %gate_scales.1, bf16[32,896]{1,0:T(8,128)(2,1)} %up_scales.1, bf16[7,4096]{1,0:T(8,128)(2,1)} %down_scales.1, s32[1024,896]{1,0:T(8,128)} %gate_hbm.1, s32[1024,896]{1,0:T(8,128)} %up_hbm.1, bf16[896,896]{1,0:T(8,128)(2,1)} %factor_hbm.1, ...), custom_call_target="tpu_custom_call" | custom-call | tf_op jit(solution)/shard_map/feed_forward/pallas_call | solution.py:521
  81.9 1.5 %copy.10 = bf16[256,128]{1,0:T(8,128)(2,1)} copy(bf16[256,128]{1,0:T(8,128)(2,1)} %feed_forward.1) | data formatting | bytes 131072

commit v3 on v1

v3 whole, which is shorter than its diff:
```python
import functools
import math

import jax
import jax.numpy as jnp
from jax import lax
from jax.experimental import pallas as pl
from jax.experimental.pallas import tpu as pltpu
from jax.sharding import PartitionSpec as P

MESH = pl.DeviceIdType.MESH
TP = 32
ROWS = 256
UNITS = 896
TILES = 7
CHUNKS = 2
CR = ROWS // CHUNKS
HALF = CR // 2
F32 = jnp.float32
BF16 = jnp.bfloat16


def field_order():
    source = lax.broadcasted_iota(jnp.int32, (128, 128), 0)
    target = lax.broadcasted_iota(jnp.int32, (128, 128), 1)
    return jnp.where(target == (source % 4) * 32 + source // 4, 1.0, 0.0).astype(BF16)


def decode(words, scale):
    flipped = jnp.bitwise_xor(words, 0x0888)
    planes = []
    for field in range(4):
        if field == 3:
            value = jnp.right_shift(words, 12)
        else:
            value = jnp.right_shift(jnp.left_shift(flipped, 28 - 4 * field), 28)
        scaled = value.astype(F32).reshape(4, 8, 128) * scale
        planes.append(scaled.reshape(32, 128).astype(BF16))
    return planes


def kernel(
    tok_in, gate_scales, up_scales, down_scales, gate_hbm, up_hbm, factor_hbm, down_hbm, out_ref,
    gate_codes, up_codes, down_codes, factor, tok, w_both, w_down, ordered, gate_f32, up_f32, down_f32, total,
    hidden, had_in, had_out, rotated, turned, part, core_in, sums, first_in, second_in, mixed, z_in,
    load_sem, tok_send, tok_recv, a_send, a_recv, b_send, b_recv, c_send, c_recv, x_send, x_recv,
    y_send, y_recv, z_send, z_recv,
):
    me = lax.axis_index("tp")
    z, x, c = me // 8, (me // 2) % 4, me % 2
    other = me + 1 - 2 * c
    right = z * 8 + ((x + 1) % 4) * 2 + c
    left = z * 8 + ((x + 3) % 4) * 2 + c
    z_of = [z, z + 1 - 2 * (z % 2), (z + 2) % 4, 3 - z]

    barrier = pltpu.get_barrier_semaphore()

    @pl.loop(1, TP)
    def _(step):
        pl.semaphore_signal(barrier, inc=1, device_id={"tp": (me + step) % TP}, device_id_type=MESH)

    def column(shift):
        return (x + shift) % 4

    def code_rows(shift, z_at):
        return pl.ds(pl.multiple_of((z_at * 4 + column(shift)) * 64, 64), 64)

    loads = {}
    for place, shift in enumerate((0, 1, 3, 2)):
        for z_at in range(4):
            rows = code_rows(shift, z_at)
            first = (place * 4 + z_at) * 2
            loads[shift, z_at] = [
                pltpu.make_async_copy(gate_hbm.at[rows], gate_codes.at[rows], load_sem.at[first]),
                pltpu.make_async_copy(up_hbm.at[rows], up_codes.at[rows], load_sem.at[first + 1]),
            ]
            for copy in loads[shift, z_at]:
                copy.start()
    factor_load = pltpu.make_async_copy(factor_hbm, factor, load_sem.at[32])
    factor_load.start()
    down_load = pltpu.make_async_copy(down_hbm, down_codes, load_sem.at[33])
    down_load.start()

    order = field_order()

    def tokens_of(block, row, count):
        lanes = pl.ds(pl.multiple_of((block // 8) * 256 + (block % 2) * 128, 128), 128)
        return tok.at[(block // 2) % 4, pl.ds(row, count), lanes]

    tokens_of(me, 0, ROWS)[...] = jnp.dot(tok_in[...], order, preferred_element_type=F32).astype(BF16)

    pl.semaphore_wait(barrier, TP - 1)

    waiting = []

    def remote(src, dst, send, recv, device):
        copy = pltpu.make_async_remote_copy(
            src_ref=src, dst_ref=dst, send_sem=send, recv_sem=recv,
            device_id={"tp": device}, device_id_type=MESH,
        )
        copy.start()
        waiting.append(copy)
        return copy

    def pass_on(block, device, row=0, count=ROWS):
        where = tokens_of(block, row, count)
        remote(where, where, tok_send.at[len(waiting)], tok_recv.at[block, 1 if row else 0], device)

    def arrived(block, row=0, count=ROWS):
        where = tokens_of(block, row, count)
        pltpu.make_async_copy(where, where, tok_recv.at[block, 1 if row else 0]).wait()

    def at(near, shift):
        return z_of[near] * 8 + column(shift) * 2 + c

    def from_z(near):
        if near:
            arrived(at(near, 0))
        pass_on(at(near, 0), right)
        pass_on(at(near, 0), left)
        if not near:
            for peer in (1, 2, 3):
                pass_on(me, at(peer, 0))
        pass_on(at(near, 0), other)

    def from_x(near):
        block = at(near, 3)
        arrived(block)
        pass_on(block, right, 0, ROWS // 2)
        pass_on(block, other)
        block = at(near, 1)
        arrived(block)
        pass_on(block, left, ROWS // 2, ROWS // 2)
        pass_on(block, other)

    def from_far(near):
        block = at(near, 2)
        arrived(block, 0, ROWS // 2)
        arrived(block, ROWS // 2, ROWS // 2)
        pass_on(block, other)

    def from_core(shift):
        for z_at in range(4):
            arrived(z_at * 8 + column(shift) * 2 + 1 - c)

    def decode_piece(shift, z_at):
        for copy in loads[shift, z_at]:
            copy.wait()

        @pl.loop(0, 2)
        def _(side):
            group = (z_at * 4 + column(shift)) * 2 + side
            rows = pl.ds(pl.multiple_of(group * 32, 32), 32)
            for tile in range(TILES):
                cols = pl.ds(128 * tile, 128)
                for place, codes, scales in ((0, gate_codes, gate_f32), (128, up_codes, up_f32)):
                    planes = decode(codes[rows, cols], scales[group, :, cols])
                    for field, plane in enumerate(planes):
                        to = pl.ds(pl.multiple_of(z_at * 256 + side * 128 + 32 * field, 32), 32)
                        w_both[column(shift), tile, to, pl.ds(place, 128)] = plane

    def product(shift, tile):
        return jnp.dot(tok[column(shift)], w_both[column(shift), tile], preferred_element_type=F32)

    chip = me // 2
    wide, narrow = pl.ds(0, 256), pl.ds(0, 128)
    group_cols = [pl.ds(0, 256), pl.ds(256, 256), pl.ds(512, 256), pl.ds(768, 128)]
    group_width = [256, 256, 256, 128]

    def scatter(group):
        side, lanes = group % 2, pl.ds(0, group_width[group])

        def give(to_chip):
            pltpu.make_async_remote_copy(
                src_ref=hidden.at[to_chip, :, group_cols[group]], dst_ref=had_in.at[group // 2, me, :, lanes],
                send_sem=a_send.at[group], recv_sem=a_recv.at[group // 2],
                device_id={"tp": to_chip * 2 + side}, device_id_type=MESH,
            ).start()

        @pl.loop(1, 16)
        def _(step):
            give((chip + 1 + (step + 2) % 15) % 16)

        @pl.when(c == side)
        def _():
            pltpu.make_async_copy(
                hidden.at[chip, :, group_cols[group]], had_in.at[group // 2, me, :, lanes], a_recv.at[group // 2]
            ).start()

        @pl.when(c != side)
        def _():
            give(chip)

    def rotate(group):
        turn, lanes = group // 2, pl.ds(0, group_width[group])
        everything = had_in.at[turn, :, :, lanes]
        pltpu.make_async_copy(everything, everything, a_recv.at[turn]).wait()
        for tile in range(group_width[group] // 128):
            cols = pl.ds(128 * tile, 128)
            held = [had_in[turn, source, :, cols].astype(F32) * (1.0 / TP) for source in range(TP)]
            apart = 1
            while apart < TP:
                held = [
                    held[i - apart] - held[i] if i & apart else held[i] + held[i + apart]
                    for i in range(TP)
                ]
                apart *= 2
            for target in range(TP):
                had_out[turn, target, :, cols] = held[target].astype(BF16)

        @pl.loop(1, TP)
        def _(step):
            device = (me + 1 + (step + 6) % (TP - 1)) % TP
            pltpu.make_async_remote_copy(
                src_ref=had_out.at[turn, device, :, lanes], dst_ref=rotated.at[chip, :, group_cols[group]],
                send_sem=b_send.at[turn], recv_sem=b_recv.at[group],
                device_id={"tp": device}, device_id_type=MESH,
            ).start()

        pltpu.make_async_copy(
            had_out.at[turn, me, :, lanes], rotated.at[chip, :, group_cols[group]], b_recv.at[group]
        ).start()

    def rotate_turn(turn):
        for side in range(2):
            @pl.when(c == side)
            def _():
                rotate(2 * turn + side)

    def back(group):
        everything = rotated.at[:, :, group_cols[group]]
        pltpu.make_async_copy(everything, everything, b_recv.at[group]).wait()

    def decode_down(first, stop):
        @pl.loop(first, stop)
        def _(place):
            for group in range(TILES):
                for side in range(2):
                    cols = pl.ds(pl.multiple_of(place * 256 + 128 * side, 128), 128)
                    planes = decode(down_codes[pl.ds(32 * group, 32), cols], down_f32[group, :, cols])
                    for field, plane in enumerate(planes):
                        to = pl.ds(pl.multiple_of((place // 4) * 256 + 128 * side, 128), 128)
                        w_down[place % 4, pl.ds(128 * group + 32 * field, 32), to] = plane

    from_other = {}

    def down(shift):
        place = column(shift)
        for pair in range(2):
            both = jnp.dot(
                turned[...], w_down[place, :, pl.ds(512 * pair, 512)], preferred_element_type=F32
            ).astype(BF16)
            for chunk in range(CHUNKS):
                rows = slice(chunk * CR, (chunk + 1) * CR)
                for z_at in range(2):
                    for side in range(2):
                        lanes = slice(256 * z_at + 128 * side, 256 * z_at + 128 * side + 128)
                        part[chunk, side, place, 2 * pair + z_at] = both[rows, lanes]
        for chunk in range(CHUNKS):
            from_other[chunk, shift] = remote(
                part.at[chunk, 1 - c, place], core_in.at[chunk, shift],
                c_send.at[chunk, shift], c_recv.at[chunk, shift], other,
            )

    top, bottom = pl.ds(0, HALF), pl.ds(HALF, HALF)

    def join(chunk, shift, rows):
        return part[chunk, c, column(shift), :, rows].astype(F32) + core_in[chunk, shift, :, rows].astype(F32)

    x_copies = {}

    def x_first(chunk):
        from_other[chunk, 2].wait_recv()
        sums[chunk, 2] = join(chunk, 2, pl.ds(0, CR)).astype(BF16)
        x_copies[chunk, "r1"] = remote(
            sums.at[chunk, 2, :, top], first_in.at[chunk, 0], x_send.at[chunk, 0], x_recv.at[chunk, 0], right
        )
        x_copies[chunk, "l1"] = remote(
            sums.at[chunk, 2, :, bottom], first_in.at[chunk, 1], x_send.at[chunk, 1], x_recv.at[chunk, 1], left
        )

    def x_second(chunk):
        from_other[chunk, 1].wait_recv()
        sums[chunk, 1, :, bottom] = join(chunk, 1, bottom).astype(BF16)
        x_copies[chunk, "r1"].wait_recv()
        sums[chunk, 1, :, top] = (join(chunk, 1, top) + first_in[chunk, 0].astype(F32)).astype(BF16)
        x_copies[chunk, "r2"] = remote(
            sums.at[chunk, 1], second_in.at[chunk, 0], y_send.at[chunk, 0], y_recv.at[chunk, 0], right
        )
        from_other[chunk, 3].wait_recv()
        sums[chunk, 3, :, top] = join(chunk, 3, top).astype(BF16)
        x_copies[chunk, "l1"].wait_recv()
        sums[chunk, 3, :, bottom] = (join(chunk, 3, bottom) + first_in[chunk, 1].astype(F32)).astype(BF16)
        x_copies[chunk, "l2"] = remote(
            sums.at[chunk, 3], second_in.at[chunk, 1], y_send.at[chunk, 1], y_recv.at[chunk, 1], left
        )

    z_copies = {}

    def z_first(chunk):
        from_other[chunk, 0].wait_recv()
        x_copies[chunk, "r2"].wait_recv()
        x_copies[chunk, "l2"].wait_recv()
        for near in (3, 2, 1, 0):
            to = z_of[near]
            value = (
                part[chunk, c, x, to].astype(F32) + core_in[chunk, 0, to].astype(F32)
                + second_in[chunk, 0, to].astype(F32) + second_in[chunk, 1, to].astype(F32)
            )
            mixed[chunk, near] = value.astype(BF16)
            if near:
                z_copies[chunk, near] = remote(
                    mixed.at[chunk, near], z_in.at[chunk, near], z_send.at[chunk, near], z_recv.at[chunk, near],
                    to * 8 + x * 2 + c,
                )

    def z_last(chunk):
        total = mixed[chunk, 0].astype(F32)
        for near in (1, 2, 3):
            z_copies[chunk, near].wait_recv()
            total = total + z_in[chunk, near].astype(F32)
        out_ref[pl.ds(chunk * CR, CR), :] = total.astype(BF16)

    from_z(0)
    for source, spread, groups in ((gate_scales, gate_f32, 32), (up_scales, up_f32, 32), (down_scales, down_f32, 7)):
        scales = source[...].astype(F32)
        for group in range(groups):
            spread[group] = jnp.broadcast_to(scales[group : group + 1], spread.shape[1:])
    for z_at in range(4):
        decode_piece(0, z_at)
    from_z(1)
    from_x(0)
    decode_piece(1, 0)
    decode_piece(1, 1)
    from_z(2)
    from_x(1)
    decode_piece(1, 2)
    decode_piece(1, 3)
    from_z(3)
    from_x(2)
    from_far(0)
    decode_piece(3, 0)
    decode_piece(3, 1)
    from_far(1)
    from_x(3)
    decode_piece(3, 2)
    decode_piece(3, 3)
    from_far(2)
    from_core(0)

    @pl.loop(0, TILES)
    def _(tile):
        total[tile] = product(0, tile)

    from_far(3)
    for z_at in range(4):
        decode_piece(2, z_at)
    factor_load.wait()
    for tile in range(TILES):
        cols = pl.ds(128 * tile, 128)
        ordered[:, cols] = jnp.dot(factor[:, cols], order, preferred_element_type=F32).astype(BF16)
    from_core(1)
    from_core(3)

    @pl.loop(0, TILES)
    def _(tile):
        total[tile] += product(1, tile) + product(3, tile)

    from_core(2)
    for group in range(4):
        @pl.loop(2 * group, min(2 * group + 2, TILES))
        def _(tile):
            both = total[tile] + product(2, tile)
            gate, up = both[:, :128], both[:, 128:]
            value = gate / (1.0 + jnp.exp(-gate)) * up
            lanes = pl.ds(pl.multiple_of(tile * 128, 128), 128)
            hidden[:, :, lanes] = value.astype(BF16).reshape(16, 16, 128)

        scatter(group)

    down_load.wait()
    decode_down(0, 8)
    rotate_turn(0)
    decode_down(8, 16)
    rotate_turn(1)
    back(0)
    back(1)
    first_part = jnp.dot(
        rotated[:, :, pl.ds(0, 512)].reshape(ROWS, 512), ordered[pl.ds(0, 512), :], preferred_element_type=F32
    )
    back(2)
    back(3)
    whole = first_part + jnp.dot(
        rotated[:, :, pl.ds(512, 384)].reshape(ROWS, 384), ordered[pl.ds(512, 384), :], preferred_element_type=F32
    )
    turned[...] = (whole * math.sqrt(TP)).astype(BF16)
    down(2)
    down(1)
    x_first(0)
    x_first(1)
    down(3)
    down(0)
    x_second(0)
    x_second(1)
    z_first(0)
    z_first(1)
    z_last(0)
    z_last(1)

    for copy in waiting:
        copy.wait_send()
    for group in range(4):
        for kept in range(2):
            @pl.when((c == group % 2) if kept else (c != group % 2))
            def _():
                sent = hidden.at[pl.ds(0, 16 - kept), :, group_cols[group]]
                pltpu.make_async_copy(sent, sent, a_send.at[group]).wait()
                if kept:
                    sent = had_out.at[group // 2, pl.ds(0, TP - 1), :, pl.ds(0, group_width[group])]
                    pltpu.make_async_copy(sent, sent, b_send.at[group // 2]).wait()


def shards(tokens, gate_codes, gate_scales, up_codes, up_scales, local_factor, down_codes, down_scales):
    vmem, hbm, dma = pl.BlockSpec(memory_space=pltpu.VMEM), pl.BlockSpec(memory_space=pl.ANY), pltpu.SemaphoreType.DMA
    return pl.pallas_call(
        kernel,
        out_shape=jax.ShapeDtypeStruct((ROWS, 128), BF16),
        in_specs=[vmem] * 4 + [hbm] * 4,
        out_specs=vmem,
        scratch_shapes=[
            pltpu.VMEM((1024, UNITS), jnp.int32),
            pltpu.VMEM((1024, UNITS), jnp.int32),
            pltpu.VMEM((224, 4096), jnp.int32),
            pltpu.VMEM((UNITS, UNITS), BF16),
            pltpu.VMEM((4, ROWS, 1024), BF16),
            pltpu.VMEM((4, TILES, 1024, 256), BF16),
            pltpu.VMEM((4, UNITS, 1024), BF16),
            pltpu.VMEM((UNITS, UNITS), BF16),
            pltpu.VMEM((32, 8, UNITS), F32),
            pltpu.VMEM((32, 8, UNITS), F32),
            pltpu.VMEM((7, 8, 4096), F32),
            pltpu.VMEM((TILES, ROWS, 256), F32),
            pltpu.VMEM((16, 16, UNITS), BF16),
            pltpu.VMEM((2, TP, 16, 256), BF16),
            pltpu.VMEM((2, TP, 16, 256), BF16),
            pltpu.VMEM((16, 16, UNITS), BF16),
            pltpu.VMEM((ROWS, UNITS), BF16),
            pltpu.VMEM((CHUNKS, 2, 4, 4, CR, 128), BF16),
            pltpu.VMEM((CHUNKS, 4, 4, CR, 128), BF16),
            pltpu.VMEM((CHUNKS, 4, 4, CR, 128), BF16),
            pltpu.VMEM((CHUNKS, 2, 4, HALF, 128), BF16),
            pltpu.VMEM((CHUNKS, 2, 4, CR, 128), BF16),
            pltpu.VMEM((CHUNKS, 4, CR, 128), BF16),
            pltpu.VMEM((CHUNKS, 4, CR, 128), BF16),
            dma((34,)),
            dma((48,)),
            dma((TP, 2)),
            dma((4,)),
            dma((2,)),
            dma((2,)),
            dma((4,)),
            dma((CHUNKS, 4)),
            dma((CHUNKS, 4)),
            dma((CHUNKS, 2)),
            dma((CHUNKS, 2)),
            dma((CHUNKS, 2)),
            dma((CHUNKS, 2)),
            dma((CHUNKS, 4)),
            dma((CHUNKS, 4)),
        ],
        compiler_params=pltpu.CompilerParams(
            collective_id=0, has_side_effects=True, vmem_limit_bytes=58 * 1024 * 1024
        ),
        name="feed_forward",
    )(tokens, gate_scales, up_scales, down_scales, gate_codes, up_codes, local_factor, down_codes)


def solution(mesh):
    return jax.shard_map(
        shards,
        mesh=mesh,
        in_specs=(
            P("req", "tp"),
            P(None, "tp"),
            P(None, "tp"),
            P(None, "tp"),
            P(None, "tp"),
            P(),
            P("tp", None),
            P("tp", None),
        ),
        out_specs=P("req", "tp"),
        check_vma=False,
    )
```

time: 78.6 us -> 73.1 us (0.930)
  Pallas kernels: 76.9 us -> 71.5 us
    pallas_call x1, Pallas kernels: 76.9 us -> 71.5 us  [shards(): pl.pallas_call(kernel, out_shape=jax.ShapeDtypeStruct((ROWS, 128), BF16),...]
where the time goes in v3:
time: 73.1 us; the launch traced here: 73 us
  Pallas kernels  71.5 us (98%)
  local copies, waits for them, and re-layouts  1.47 us (2%)
    pallas_call x1, Pallas kernels, shards(): pl.pallas_call(kernel, out_shape=jax.ShapeDtypeStruct((ROWS, 128), BF16),...  71.5 us
    unnamed x1, local copies, waits for them, and re-layouts  1.47 us

profile of v3, /device:TPU:16, one launch (start us, length us, event | category | flops | bytes accessed | tf_op | source)
XLA Modules:
  0.0 73.0 jit_solution(14984628716098175852)
XLA Ops:
  0.0 71.5 %feed_forward.1 = bf16[256,128]{1,0:T(8,128)(2,1)} custom-call(bf16[256,128]{1,0:T(8,128)(2,1)} %tok_in.1, bf16[32,896]{1,0:T(8,128)(2,1)} %gate_scales.1, bf16[32,896]{1,0:T(8,128)(2,1)} %up_scales.1, bf16[7,4096]{1,0:T(8,128)(2,1)} %down_scales.1, s32[1024,896]{1,0:T(8,128)} %gate_hbm.1, s32[1024,896]{1,0:T(8,128)} %up_hbm.1, bf16[896,896]{1,0:T(8,128)(2,1)} %factor_hbm.1, ...), custom_call_target="tpu_custom_call" | custom-call | tf_op jit(solution)/shard_map/feed_forward/pallas_call | solution.py:425
  71.5 1.5 %copy.10 = bf16[256,128]{1,0:T(8,128)(2,1)} copy(bf16[256,128]{1,0:T(8,128)(2,1)} %feed_forward.1) | data formatting | bytes 131072

commit v4 on v0

v4 whole, which is shorter than its diff:
```python
import functools
import math

import jax
import jax.numpy as jnp
from jax import lax
from jax.experimental import pallas as pl
from jax.experimental.pallas import tpu as pltpu
from jax.sharding import PartitionSpec as P

MESH = pl.DeviceIdType.MESH
TP = 32
ROWS = 256
UNITS = 896
TILES = 7
CHUNKS = 2
CR = ROWS // CHUNKS
HALF = CR // 2
F32 = jnp.float32
BF16 = jnp.bfloat16


def field_order():
    source = lax.broadcasted_iota(jnp.int32, (128, 128), 0)
    target = lax.broadcasted_iota(jnp.int32, (128, 128), 1)
    return jnp.where(target == (source % 4) * 32 + source // 4, 1.0, 0.0).astype(BF16)


def decode(words, scale):
    flipped = jnp.bitwise_xor(words, 0x0888)
    planes = []
    for field in range(4):
        if field == 3:
            value = jnp.right_shift(words, 12)
        else:
            value = jnp.right_shift(jnp.left_shift(flipped, 28 - 4 * field), 28)
        scaled = value.astype(F32).reshape(4, 8, 128) * scale
        planes.append(scaled.reshape(32, 128).astype(BF16))
    return planes


def kernel(
    tok_in, gate_scales, up_scales, down_scales, gate_hbm, up_hbm, factor_hbm, down_hbm, out_ref,
    gate_codes, up_codes, down_codes, factor, tok, w_both, w_down, ordered, gate_f32, up_f32, down_f32, total,
    hidden, had_in, had_out, rotated, turned, part, core_in, sums, first_in, second_in, mixed, z_in,
    load_sem, own_send, near_send, x_tok_send, far_send, tok_recv, a_send, a_recv, b_send, b_recv,
    c_send, c_recv, x_send, x_recv, y_send, y_recv, z_send, z_recv,
):
    me = lax.axis_index("tp")
    z, x, c = me // 8, (me // 2) % 4, me % 2
    chip = me // 2
    other = me + 1 - 2 * c
    right = z * 8 + ((x + 1) % 4) * 2 + c
    left = z * 8 + ((x + 3) % 4) * 2 + c

    def z_of(near):
        return 2 * ((z // 2 + near // 2) % 2) + (z + near) % 2

    def column(shift):
        return (x + shift) % 4

    def use_order(place):
        return place + (place // 2) * (1 - 2 * (place % 2))

    def lanes_at(start, width):
        return pl.ds(pl.multiple_of(start, 128), width)

    def send(src, dst, send_sem, recv_sem, device):
        pltpu.make_async_remote_copy(
            src_ref=src, dst_ref=dst, send_sem=send_sem, recv_sem=recv_sem,
            device_id={"tp": device}, device_id_type=MESH,
        ).start()

    def wait(shaped, sem):
        pltpu.make_async_copy(shaped, shaped, sem).wait()

    barrier = pltpu.get_barrier_semaphore()

    @pl.loop(1, TP)
    def _(step):
        pl.semaphore_signal(barrier, inc=1, device_id={"tp": (me + step) % TP}, device_id_type=MESH)

    def code_rows(step):
        return pl.ds(pl.multiple_of(((step % 4) * 4 + column(use_order(step // 4))) * 64, 64), 64)

    @pl.loop(0, 16)
    def _(step):
        rows = code_rows(step)
        pltpu.make_async_copy(gate_hbm.at[rows], gate_codes.at[rows], load_sem.at[step]).start()
        pltpu.make_async_copy(up_hbm.at[rows], up_codes.at[rows], load_sem.at[16 + step]).start()

    pltpu.make_async_copy(factor_hbm, factor, load_sem.at[32]).start()
    pltpu.make_async_copy(down_hbm, down_codes, load_sem.at[33]).start()

    order = field_order()

    def tokens_of(block, row=0, count=ROWS):
        return tok.at[(block // 2) % 4, pl.ds(row, count), lanes_at((block // 8) * 256 + (block % 2) * 128, 128)]

    tokens_of(me)[...] = jnp.dot(tok_in[...], order, preferred_element_type=F32).astype(BF16)

    @pl.loop(0, 2)
    def _(step):
        rows = pl.ds(pl.multiple_of(step * 16, 16), 16)
        for source, spread in ((gate_scales, gate_f32), (up_scales, up_f32)):
            scales = source[rows, :].astype(F32)
            for row in range(16):
                spread[step * 16 + row] = jnp.broadcast_to(scales[row : row + 1], (8, UNITS))

    @pl.loop(0, TILES)
    def _(tile):
        total[tile] = jnp.zeros((ROWS, 256), F32)

    pl.semaphore_wait(barrier, TP - 1)

    def pass_on(block, device, sem, row=0, count=ROWS):
        where = tokens_of(block, row, count)
        send(where, where, sem, tok_recv.at[block, 1 if row else 0], device)

    def arrived(block, row=0, count=ROWS):
        wait(tokens_of(block, row, count), tok_recv.at[block, 1 if row else 0])

    def block_at(near, shift):
        return z_of(near) * 8 + column(shift) * 2 + c

    def pass_near(near):
        block = block_at(near, 0)
        pass_on(block, right, near_send.at[near, 0])
        pass_on(block, left, near_send.at[near, 1])
        pass_on(block, other, near_send.at[near, 2])

    def from_z(near):
        arrived(block_at(near, 0))
        pass_near(near)

    def from_x(near):
        block = block_at(near, 3)
        arrived(block)
        pass_on(block, right, x_tok_send.at[near, 0], 0, ROWS // 2)
        pass_on(block, other, x_tok_send.at[near, 1])
        block = block_at(near, 1)
        arrived(block)
        pass_on(block, left, x_tok_send.at[near, 2], ROWS // 2, ROWS // 2)
        pass_on(block, other, x_tok_send.at[near, 3])

    def from_far(near):
        block = block_at(near, 2)
        arrived(block, 0, ROWS // 2)
        arrived(block, ROWS // 2, ROWS // 2)
        pass_on(block, other, far_send.at[near])

    def from_core(shift):
        @pl.loop(0, 4)
        def _(z_at):
            arrived(z_at * 8 + column(shift) * 2 + 1 - c)

    def decode_half(turn):
        shift = use_order(turn // 2)

        @pl.loop(0, 4)
        def _(piece):
            z_at, side = (turn % 2) * 2 + piece // 2, piece % 2

            @pl.when(side == 0)
            def _():
                step = (turn // 2) * 4 + z_at
                wait(gate_codes.at[code_rows(step)], load_sem.at[step])
                wait(up_codes.at[code_rows(step)], load_sem.at[16 + step])

            group = (z_at * 4 + column(shift)) * 2 + side
            rows = pl.ds(pl.multiple_of(group * 32, 32), 32)
            for tile in range(TILES):
                cols = pl.ds(128 * tile, 128)
                for place, codes, scales in ((0, gate_codes, gate_f32), (128, up_codes, up_f32)):
                    planes = decode(codes[rows, cols], scales[group, :, cols])
                    for field, plane in enumerate(planes):
                        to = pl.ds(pl.multiple_of(z_at * 256 + side * 128 + 32 * field, 32), 32)
                        w_both[column(shift), tile, to, pl.ds(place, 128)] = plane

    def product(shift, tile):
        return jnp.dot(tok[column(shift)], w_both[column(shift), tile], preferred_element_type=F32)

    pass_near(0)

    @pl.loop(1, 4)
    def _(near):
        pass_on(me, block_at(near, 0), own_send.at[near])

    @pl.loop(0, 10)
    def _(turn):
        @pl.when(turn < 8)
        def _():
            decode_half(turn)

        even = turn % 2 == 0

        @pl.when(jnp.logical_and(even, turn < 6))
        def _():
            from_z(turn // 2 + 1)

        @pl.when(jnp.logical_and(turn % 2 == 1, turn < 8))
        def _():
            from_x(turn // 2)

        @pl.when(jnp.logical_and(turn % 2 == 1, turn >= 3))
        def _():
            from_far(turn // 2 - 1)

        @pl.when(jnp.logical_or(turn == 6, turn >= 8))
        def _():
            shift = (turn // 8) * (1 + 2 * (turn % 2))
            from_core(shift)

            @pl.loop(0, TILES)
            def _(tile):
                total[tile] += product(shift, tile)

    def scatter(group, width):
        side, cols, lanes = group % 2, lanes_at(group * 256, width), pl.ds(0, width)

        def give(to_chip):
            send(
                hidden.at[to_chip, :, cols], had_in.at[group // 2, me, :, lanes],
                a_send.at[group], a_recv.at[group // 2], to_chip * 2 + side,
            )

        @pl.loop(1, 16)
        def _(step):
            give((chip + 1 + (step + 2) % 15) % 16)

        @pl.when(c == side)
        def _():
            pltpu.make_async_copy(
                hidden.at[chip, :, cols], had_in.at[group // 2, me, :, lanes], a_recv.at[group // 2]
            ).start()

        @pl.when(c != side)
        def _():
            give(chip)

    from_core(2)

    @pl.loop(0, TILES)
    def _(tile):
        both = total[tile] + product(2, tile)
        gate, up = both[:, :128], both[:, 128:]
        value = gate / (1.0 + jnp.exp(-gate)) * up
        hidden[:, :, lanes_at(tile * 128, 128)] = value.astype(BF16).reshape(16, 16, 128)

        @pl.when(tile % 2 == 1)
        def _():
            scatter(tile // 2, 256)

    scatter(3, 128)

    for group in range(7):
        down_f32[group] = jnp.broadcast_to(down_scales[group : group + 1, :].astype(F32), (8, 4096))
    wait(factor, load_sem.at[32])

    @pl.loop(0, TILES)
    def _(tile):
        cols = lanes_at(tile * 128, 128)
        ordered[:, cols] = jnp.dot(factor[:, cols], order, preferred_element_type=F32).astype(BF16)

    ordered[:, pl.ds(UNITS, 128)] = jnp.zeros((UNITS, 128), BF16)
    wait(down_codes, load_sem.at[33])

    def decode_down(place):
        for group in range(TILES):
            for side in range(2):
                cols = lanes_at(place * 256 + 128 * side, 128)
                planes = decode(down_codes[pl.ds(32 * group, 32), cols], down_f32[group, :, cols])
                for field, plane in enumerate(planes):
                    to = lanes_at((place // 4) * 256 + 128 * side, 128)
                    w_down[place % 4, pl.ds(128 * group + 32 * field, 32), to] = plane

    def combine(turn, tile):
        cols = lanes_at(tile * 128, 128)
        held = [had_in[turn, source, :, cols].astype(F32) * (1.0 / TP) for source in range(TP)]
        apart = 1
        while apart < TP:
            held = [
                held[i - apart] - held[i] if i & apart else held[i] + held[i + apart]
                for i in range(TP)
            ]
            apart *= 2
        for target in range(TP):
            had_out[turn, target, :, cols] = held[target].astype(BF16)

    def give_back(turn, group, width):
        cols, lanes = lanes_at(group * 256, width), pl.ds(0, width)

        @pl.loop(1, TP)
        def _(step):
            device = (me + 1 + (step + 6) % (TP - 1)) % TP
            send(
                had_out.at[turn, device, :, lanes], rotated.at[chip, :, cols],
                b_send.at[turn], b_recv.at[group], device,
            )

        pltpu.make_async_copy(
            had_out.at[turn, me, :, lanes], rotated.at[chip, :, cols], b_recv.at[group]
        ).start()

    @pl.loop(0, 2)
    def _(turn):
        @pl.loop(8 * turn, 8 * turn + 8)
        def _(place):
            decode_down(place)

        group = 2 * turn + c

        @pl.when(group < 3)
        def _():
            wait(had_in.at[turn], a_recv.at[turn])

        @pl.when(group == 3)
        def _():
            wait(had_in.at[turn, :, :, pl.ds(0, 128)], a_recv.at[turn])

        @pl.loop(0, 2 - group // 3)
        def _(tile):
            combine(turn, tile)

        @pl.when(group < 3)
        def _():
            give_back(turn, group, 256)

        @pl.when(group == 3)
        def _():
            give_back(turn, 3, 128)

    for group, width in enumerate((256, 256, 256, 128)):
        wait(rotated.at[:, :, pl.ds(256 * group, width)], b_recv.at[group])

    @pl.loop(0, 4)
    def _(tile):
        cols = lanes_at(tile * 256, 256)
        value = jnp.dot(rotated[...].reshape(ROWS, UNITS), ordered[:, cols], preferred_element_type=F32)
        turned[:, cols] = (value * math.sqrt(TP)).astype(BF16)

    top, bottom = pl.ds(0, HALF), pl.ds(HALF, HALF)

    def join(chunk, shift, rows):
        return part[chunk, c, column(shift), :, rows].astype(F32) + core_in[chunk, shift, :, rows].astype(F32)

    def from_other(chunk, shift):
        wait(core_in.at[chunk, shift], c_recv.at[chunk, shift])

    def x_first(chunk):
        from_other(chunk, 2)
        sums[chunk, 2] = join(chunk, 2, pl.ds(0, CR)).astype(BF16)
        send(sums.at[chunk, 2, :, top], first_in.at[chunk, 0], x_send.at[chunk, 0], x_recv.at[chunk, 0], right)
        send(sums.at[chunk, 2, :, bottom], first_in.at[chunk, 1], x_send.at[chunk, 1], x_recv.at[chunk, 1], left)

    def x_second(chunk):
        from_other(chunk, 1)
        sums[chunk, 1, :, bottom] = join(chunk, 1, bottom).astype(BF16)
        wait(first_in.at[chunk, 0], x_recv.at[chunk, 0])
        sums[chunk, 1, :, top] = (join(chunk, 1, top) + first_in[chunk, 0].astype(F32)).astype(BF16)
        send(sums.at[chunk, 1], second_in.at[chunk, 0], y_send.at[chunk, 0], y_recv.at[chunk, 0], right)
        from_other(chunk, 3)
        sums[chunk, 3, :, top] = join(chunk, 3, top).astype(BF16)
        wait(first_in.at[chunk, 1], x_recv.at[chunk, 1])
        sums[chunk, 3, :, bottom] = (join(chunk, 3, bottom) + first_in[chunk, 1].astype(F32)).astype(BF16)
        send(sums.at[chunk, 3], second_in.at[chunk, 1], y_send.at[chunk, 1], y_recv.at[chunk, 1], left)

    def z_first(chunk):
        from_other(chunk, 0)
        wait(second_in.at[chunk, 0], y_recv.at[chunk, 0])
        wait(second_in.at[chunk, 1], y_recv.at[chunk, 1])

        @pl.loop(0, 4)
        def _(step):
            near = 3 - step
            to = z_of(near)
            value = (
                part[chunk, c, x, to].astype(F32) + core_in[chunk, 0, to].astype(F32)
                + second_in[chunk, 0, to].astype(F32) + second_in[chunk, 1, to].astype(F32)
            )
            mixed[chunk, near] = value.astype(BF16)

            @pl.when(near > 0)
            def _():
                send(
                    mixed.at[chunk, near], z_in.at[chunk, near], z_send.at[chunk, near], z_recv.at[chunk, near],
                    to * 8 + x * 2 + c,
                )

    def z_last(chunk):
        value = mixed[chunk, 0].astype(F32)
        for near in (1, 2, 3):
            wait(z_in.at[chunk, near], z_recv.at[chunk, near])
            value = value + z_in[chunk, near].astype(F32)
        out_ref[pl.ds(pl.multiple_of(chunk * CR, CR), CR), :] = value.astype(BF16)

    @pl.loop(0, 8)
    def _(step):
        turn, pair = step // 2, step % 2
        shift = jnp.where(turn == 3, 0, jnp.where(turn == 2, 3, 2 - turn))
        place = column(shift)
        both = jnp.dot(
            turned[:, pl.ds(0, UNITS)], w_down[place, :, lanes_at(512 * pair, 512)], preferred_element_type=F32
        ).astype(BF16)
        for chunk in range(CHUNKS):
            for z_at in range(2):
                for side in range(2):
                    lane = 256 * z_at + 128 * side
                    part[chunk, side, place, 2 * pair + z_at] = both[chunk * CR : chunk * CR + CR, lane : lane + 128]

        @pl.when(pair == 1)
        def _():
            @pl.loop(0, CHUNKS)
            def _(chunk):
                send(
                    part.at[chunk, 1 - c, place], core_in.at[chunk, shift],
                    c_send.at[chunk, shift], c_recv.at[chunk, shift], other,
                )

        @pl.when(step == 4)
        def _():
            pl.loop(0, CHUNKS)(x_first)

    pl.loop(0, CHUNKS)(x_second)
    pl.loop(0, CHUNKS)(z_first)
    pl.loop(0, CHUNKS)(z_last)

    @pl.loop(0, 4)
    def _(near):
        whole, half = tokens_of(0), tokens_of(0, 0, ROWS // 2)
        for to in range(3):
            wait(whole, near_send.at[near, to])
        for to in range(4):
            wait(whole if to % 2 else half, x_tok_send.at[near, to])
        wait(whole, far_send.at[near])

        @pl.when(near > 0)
        def _():
            wait(whole, own_send.at[near])

        @pl.loop(0, CHUNKS)
        def _(chunk):
            wait(core_in.at[chunk, near], c_send.at[chunk, near])

            @pl.when(near > 0)
            def _():
                wait(z_in.at[chunk, near], z_send.at[chunk, near])

            @pl.when(near < 2)
            def _():
                wait(first_in.at[chunk, near], x_send.at[chunk, near])
                wait(second_in.at[chunk, near], y_send.at[chunk, near])

    for group, width in enumerate((256, 256, 256, 128)):
        for kept in range(2):
            @pl.when((c == group % 2) if kept else (c != group % 2))
            def _():
                wait(hidden.at[pl.ds(0, 16 - kept), :, pl.ds(256 * group, width)], a_send.at[group])
                if kept:
                    wait(had_out.at[group // 2, pl.ds(0, TP - 1), :, pl.ds(0, width)], b_send.at[group // 2])


def shards(tokens, gate_codes, gate_scales, up_codes, up_scales, local_factor, down_codes, down_scales):
    vmem, hbm, dma = pl.BlockSpec(memory_space=pltpu.VMEM), pl.BlockSpec(memory_space=pl.ANY), pltpu.SemaphoreType.DMA
    return pl.pallas_call(
        kernel,
        out_shape=jax.ShapeDtypeStruct((ROWS, 128), BF16),
        in_specs=[vmem] * 4 + [hbm] * 4,
        out_specs=vmem,
        scratch_shapes=[
            pltpu.VMEM((1024, UNITS), jnp.int32),
            pltpu.VMEM((1024, UNITS), jnp.int32),
            pltpu.VMEM((224, 4096), jnp.int32),
            pltpu.VMEM((UNITS, UNITS), BF16),
            pltpu.VMEM((4, ROWS, 1024), BF16),
            pltpu.VMEM((4, TILES, 1024, 256), BF16),
            pltpu.VMEM((4, UNITS, 1024), BF16),
            pltpu.VMEM((UNITS, 1024), BF16),
            pltpu.VMEM((32, 8, UNITS), F32),
            pltpu.VMEM((32, 8, UNITS), F32),
            pltpu.VMEM((7, 8, 4096), F32),
            pltpu.VMEM((TILES, ROWS, 256), F32),
            pltpu.VMEM((16, 16, UNITS), BF16),
            pltpu.VMEM((2, TP, 16, 256), BF16),
            pltpu.VMEM((2, TP, 16, 256), BF16),
            pltpu.VMEM((16, 16, UNITS), BF16),
            pltpu.VMEM((ROWS, 1024), BF16),
            pltpu.VMEM((CHUNKS, 2, 4, 4, CR, 128), BF16),
            pltpu.VMEM((CHUNKS, 4, 4, CR, 128), BF16),
            pltpu.VMEM((CHUNKS, 4, 4, CR, 128), BF16),
            pltpu.VMEM((CHUNKS, 2, 4, HALF, 128), BF16),
            pltpu.VMEM((CHUNKS, 2, 4, CR, 128), BF16),
            pltpu.VMEM((CHUNKS, 4, CR, 128), BF16),
            pltpu.VMEM((CHUNKS, 4, CR, 128), BF16),
            dma((34,)),
            dma((4,)),
            dma((4, 3)),
            dma((4, 4)),
            dma((4,)),
            dma((TP, 2)),
            dma((4,)),
            dma((2,)),
            dma((2,)),
            dma((4,)),
            dma((CHUNKS, 4)),
            dma((CHUNKS, 4)),
            dma((CHUNKS, 2)),
            dma((CHUNKS, 2)),
            dma((CHUNKS, 2)),
            dma((CHUNKS, 2)),
            dma((CHUNKS, 4)),
            dma((CHUNKS, 4)),
        ],
        compiler_params=pltpu.CompilerParams(
            collective_id=0, has_side_effects=True, vmem_limit_bytes=58 * 1024 * 1024
        ),
        name="feed_forward",
    )(tokens, gate_scales, up_scales, down_scales, gate_codes, up_codes, local_factor, down_codes)


def solution(mesh):
    return jax.shard_map(
        shards,
        mesh=mesh,
        in_specs=(
            P("req", "tp"),
            P(None, "tp"),
            P(None, "tp"),
            P(None, "tp"),
            P(None, "tp"),
            P(),
            P("tp", None),
            P("tp", None),
        ),
        out_specs=P("req", "tp"),
        check_vma=False,
    )
```

time: 345 us -> 75.8 us (0.22)
  waiting for transfers between devices: 181 us -> 0 us
  local copies, waits for them, and re-layouts: 80.8 us -> 1.47 us
  Pallas kernels: 0 us -> 74.2 us
  other arithmetic: 39.8 us -> 0 us
  matrix products: 17.8 us -> 0 us
  between operations: 13.5 us -> 0.01 us
  starting transfers between devices: 9.91 us -> 0 us
    unnamed x3 -> x0, waiting for transfers between devices: 148 us -> none
    shift_right_arithmetic x10 -> x0, local copies, waits for them, and re-layouts: 75.1 us -> none  [unpack(): nibble = jnp.bitwise_and(jnp.right_shift(lifted[:, None, :], shifts), 15)]
    pallas_call x0 -> x1, Pallas kernels: none -> 74.2 us  [shards(): pl.pallas_call(kernel, out_shape=jax.ShapeDtypeStruct((ROWS, 128), BF16),...]
    ppermute x5 -> x0, waiting for transfers between devices: 32.6 us -> none  [from_partner(): return lax.ppermute(value, axis, pairs)]
    convert_element_type x9 -> x0, other arithmetic: 31 us -> none  [the longest x2 27.2 us: unpack(): return values.reshape(row_count, col_count).astype(jnp.bfloat16)]
    dot_general x3 -> x0, matrix products: 17.8 us -> none  [the longest x1 9.99 us: shards(): jnp.dot(lax.all_gather(tokens, 'tp', axis=1, tiled=True), w_both, preferr...]
    ppermute x5 -> x0, starting transfers between devices: 9.87 us -> none  [from_partner(): return lax.ppermute(value, axis, pairs)]
    add x3 -> x0, other arithmetic: 8.83 us -> none  [unpack(): lifted = packed + 32768]
  transfers between devices with their start and end apart: 7 -> 0, of which waited for: 5 -> 0; matrix products, arithmetic and copies ran while one was open for 32% -> 0% of each run, Pallas kernels for 0% -> 0%
where the time goes in v4:
time: 75.8 us; the launch traced here: 75.7 us
  Pallas kernels  74.2 us (98%)
  local copies, waits for them, and re-layouts  1.47 us (2%)
    pallas_call x1, Pallas kernels, shards(): pl.pallas_call(kernel, out_shape=jax.ShapeDtypeStruct((ROWS, 128), BF16),...  74.2 us

profile of v4, /device:TPU:16, one launch (start us, length us, event | category | flops | bytes accessed | tf_op | source)
XLA Modules:
  0.0 75.7 jit_solution(17695967138727178124)
XLA Ops:
  0.0 74.2 %feed_forward.1 = bf16[256,128]{1,0:T(8,128)(2,1)} custom-call(bf16[256,128]{1,0:T(8,128)(2,1)} %tok_in.1, bf16[32,896]{1,0:T(8,128)(2,1)} %gate_scales.1, bf16[32,896]{1,0:T(8,128)(2,1)} %up_scales.1, bf16[7,4096]{1,0:T(8,128)(2,1)} %down_scales.1, s32[1024,896]{1,0:T(8,128)} %gate_hbm.1, s32[1024,896]{1,0:T(8,128)} %up_hbm.1, bf16[896,896]{1,0:T(8,128)(2,1)} %factor_hbm.1, ...), custom_call_target="tpu_custom_call" | custom-call | tf_op jit(solution)/shard_map/feed_forward/pallas_call | solution.py:465
  74.2 1.5 %copy.10 = bf16[256,128]{1,0:T(8,128)(2,1)} copy(bf16[256,128]{1,0:T(8,128)(2,1)} %feed_forward.1) | data formatting | bytes 131072

commit v5 on v2

v5 whole, which is shorter than its diff:
```python
import functools
import math

import jax
import jax.numpy as jnp
from jax import lax
from jax.experimental import pallas as pl
from jax.experimental.pallas import tpu as pltpu
from jax.sharding import PartitionSpec as P

MESH = pl.DeviceIdType.MESH
TP = 32
ROWS = 256
UNITS = 896
TILES = 7
CHUNKS = 2
CR = ROWS // CHUNKS
HALF = CR // 2
F32 = jnp.float32
BF16 = jnp.bfloat16


def field_order():
    source = lax.broadcasted_iota(jnp.int32, (128, 128), 0)
    target = lax.broadcasted_iota(jnp.int32, (128, 128), 1)
    return jnp.where(target == (source % 4) * 32 + source // 4, 1.0, 0.0).astype(BF16)


def decode(words, scale):
    flipped = jnp.bitwise_xor(words, 0x0888)
    planes = []
    for field in range(4):
        if field == 3:
            value = jnp.right_shift(words, 12)
        else:
            value = jnp.right_shift(jnp.left_shift(flipped, 28 - 4 * field), 28)
        scaled = value.astype(F32).reshape(4, 8, 128) * scale
        planes.append(scaled.reshape(32, 128).astype(BF16))
    return planes


def kernel(
    tok_in, gate_scales, up_scales, down_scales, gate_hbm, up_hbm, factor_hbm, down_hbm, out_ref,
    gate_codes, up_codes, down_codes, factor, tok, w_both, w_down, ordered, gate_f32, up_f32, down_f32,
    hidden, had_in, had_out, rotated, turned, part, core_in, sums, first_in, second_in, mixed, z_in,
    load_sem, tok_send, tok_recv, a_send, a_recv, b_send, b_recv, c_send, c_recv, x_send, x_recv,
    y_send, y_recv, z_send, z_recv,
):
    me = lax.axis_index("tp")
    z, x, c = me // 8, (me // 2) % 4, me % 2
    other = me + 1 - 2 * c
    right = z * 8 + ((x + 1) % 4) * 2 + c
    left = z * 8 + ((x + 3) % 4) * 2 + c
    z_of = [z, z + 1 - 2 * (z % 2), (z + 2) % 4, 3 - z]

    def here(device):
        return {"tp": device}

    barrier = pltpu.get_barrier_semaphore()

    @pl.loop(1, TP)
    def _(step):
        pl.semaphore_signal(barrier, inc=1, device_id=here((me + step) % TP), device_id_type=MESH)

    loads = []
    for piece in range(4):
        rows = pl.ds(256 * piece, 256)
        loads.append([
            pltpu.make_async_copy(gate_hbm.at[rows], gate_codes.at[rows], load_sem.at[piece]),
            pltpu.make_async_copy(up_hbm.at[rows], up_codes.at[rows], load_sem.at[4 + piece]),
        ])
        for copy in loads[-1]:
            copy.start()
    factor_load = pltpu.make_async_copy(factor_hbm, factor, load_sem.at[8])
    factor_load.start()
    down_load = pltpu.make_async_copy(down_hbm, down_codes, load_sem.at[9])
    down_load.start()

    order = field_order()

    def column(shift):
        return (x + shift) % 4

    def columns(block):
        return pl.ds(pl.multiple_of(block * 128, 128), 128)

    tok[:, columns(me)] = jnp.dot(tok_in[...], order, preferred_element_type=F32).astype(BF16)

    def spread_scales(source, spread, groups):
        scales = source[...].astype(F32)
        for group in range(groups):
            spread[group] = jnp.broadcast_to(scales[group : group + 1], spread.shape[1:])

    def decode_piece(piece):
        if piece % 2 == 0:
            for copy in loads[piece // 2]:
                copy.wait()

        @pl.loop(4 * piece, 4 * piece + 4)
        def _(group):
            rows = pl.ds(pl.multiple_of(group * 32, 32), 32)
            for tile in range(TILES):
                cols = pl.ds(128 * tile, 128)
                for place, codes, scales in ((0, gate_codes, gate_f32), (128, up_codes, up_f32)):
                    planes = decode(codes[rows, cols], scales[group, :, cols])
                    for field, plane in enumerate(planes):
                        to = pl.ds(pl.multiple_of(group * 128 + 32 * field, 32), 32)
                        w_both[tile, to, pl.ds(place, 128)] = plane

    spread_scales(gate_scales, gate_f32, 32)
    spread_scales(up_scales, up_f32, 32)
    decode_piece(0)

    pl.semaphore_wait(barrier, TP - 1)

    waiting = []

    def remote(src, dst, send, recv, device):
        copy = pltpu.make_async_remote_copy(
            src_ref=src, dst_ref=dst, send_sem=send, recv_sem=recv, device_id=device, device_id_type=MESH,
        )
        copy.start()
        waiting.append(copy)
        return copy

    def rows_of(chunk, part):
        if part is None:
            return pl.ds(chunk * CR, CR)
        return pl.ds(chunk * CR + part * HALF, HALF)

    def slot(chunk, block, part):
        return tok_recv.at[chunk, block, part or 0]

    def pass_on(chunk, block, device, part=None):
        where = tok.at[rows_of(chunk, part), columns(block)]
        remote(where, where, tok_send.at[len(waiting)], slot(chunk, block, part), here(device))

    def arrived(chunk, block, part=None):
        where = tok.at[rows_of(chunk, part), columns(block)]
        pltpu.make_async_copy(where, where, slot(chunk, block, part)).wait()

    def at(near, shift):
        return z_of[near] * 8 + ((x + shift) % 4) * 2 + c

    def send_own(chunk):
        for near in (1, 2, 3):
            pass_on(chunk, me, at(near, 0))

    def from_z(chunk, near):
        block = at(near, 0)
        if near:
            arrived(chunk, block)
        pass_on(chunk, block, right)
        pass_on(chunk, block, left)
        pass_on(chunk, block, other)

    def from_x(chunk, near):
        block = at(near, 3)
        arrived(chunk, block)
        pass_on(chunk, block, right, 0)
        pass_on(chunk, block, other)
        block = at(near, 1)
        arrived(chunk, block)
        pass_on(chunk, block, left, 1)
        pass_on(chunk, block, other)

    def from_far(chunk, near):
        block = at(near, 2)
        arrived(chunk, block, 0)
        arrived(chunk, block, 1)
        pass_on(chunk, block, other)

    def from_core(chunk):
        @pl.loop(0, TP // 2)
        def _(chip):
            arrived(chunk, chip * 2 + 1 - c)

    def gate_up(chunk, first, stop):
        for tile in range(first, stop):
            rows = rows_of(chunk, None)
            both = jnp.dot(tok[rows, :], w_both[tile], preferred_element_type=F32)
            gate, up = both[:, :128], both[:, 128:]
            value = gate / (1.0 + jnp.exp(-gate)) * up
            hidden[pl.ds(8 * chunk, 8), :, pl.ds(128 * tile, 128)] = value.astype(BF16).reshape(8, 16, 128)

    group_cols = [pl.ds(0, 256), pl.ds(256, 256), pl.ds(512, 256), pl.ds(768, 128)]
    group_width = [256, 256, 256, 128]

    row_tile = z * 2 + x // 2

    def scatter(chunk, group):
        side, lanes = group % 2, pl.ds(0, group_width[group])
        parity = (group // 2 + chunk) % 2

        def give(step):
            dz, half = (z + 1 + step // 2) % 4, (x // 2 + step) % 2
            device, tile = dz * 8 + (parity + 2 * half) * 2 + side, chunk * 8 + dz * 2 + half
            pltpu.make_async_remote_copy(
                src_ref=hidden.at[tile, :, group_cols[group]], dst_ref=had_in.at[chunk, me, :, lanes],
                send_sem=a_send.at[group], recv_sem=a_recv.at[chunk],
                device_id=here(device), device_id_type=MESH,
            ).start()

        for step in range(6):
            give(step)
        give(7)
        own = jnp.logical_and(c == side, x % 2 == parity)

        @pl.when(own)
        def _():
            pltpu.make_async_copy(
                hidden.at[chunk * 8 + row_tile, :, group_cols[group]], had_in.at[chunk, me, :, lanes],
                a_recv.at[chunk],
            ).start()

        @pl.when(jnp.logical_not(own))
        def _():
            give(6)

    def my_group(chunk):
        return 2 * ((x + chunk) % 2) + c

    def rotate_part(chunk, width, to_cols):
        lanes = pl.ds(0, width)
        everything = had_in.at[chunk, :, :, lanes]
        pltpu.make_async_copy(everything, everything, a_recv.at[chunk]).wait()
        for tile in range(width // 128):
            cols = pl.ds(128 * tile, 128)
            held = [had_in[chunk, source, :, cols].astype(F32) * (1.0 / TP) for source in range(TP)]
            apart = 1
            while apart < TP:
                held = [
                    held[i - apart] - held[i] if i & apart else held[i] + held[i + apart]
                    for i in range(TP)
                ]
                apart *= 2
            for target in range(TP):
                had_out[chunk, target, :, cols] = held[target].astype(BF16)

        @pl.loop(1, TP)
        def _(step):
            device = (me + 1 + (step + 6) % (TP - 1)) % TP
            pltpu.make_async_remote_copy(
                src_ref=had_out.at[chunk, device, :, lanes], dst_ref=rotated.at[chunk * 8 + row_tile, :, to_cols],
                send_sem=b_send.at[chunk], recv_sem=b_recv.at[chunk],
                device_id=here(device), device_id_type=MESH,
            ).start()

        pltpu.make_async_copy(
            had_out.at[chunk, me, :, lanes], rotated.at[chunk * 8 + row_tile, :, to_cols], b_recv.at[chunk]
        ).start()

    def rotate(chunk):
        group = my_group(chunk)

        @pl.when(group < 3)
        def _():
            rotate_part(chunk, 256, pl.ds(pl.multiple_of(group * 256, 256), 256))

        @pl.when(group == 3)
        def _():
            rotate_part(chunk, 128, group_cols[3])

    def turn(chunk):
        tiles = pl.ds(8 * chunk, 8)
        everything = rotated.at[tiles]
        pltpu.make_async_copy(everything, everything, b_recv.at[chunk]).wait()
        value = jnp.dot(rotated[tiles].reshape(CR, UNITS), ordered[...], preferred_element_type=F32)
        turned[pl.ds(chunk * CR, CR), :] = (value * math.sqrt(TP)).astype(BF16)

    def decode_down(first, stop):
        @pl.loop(first, stop)
        def _(place):
            for group in range(TILES):
                for side in range(2):
                    cols = pl.ds(pl.multiple_of(place * 256 + 128 * side, 128), 128)
                    planes = decode(down_codes[pl.ds(32 * group, 32), cols], down_f32[group, :, cols])
                    for field, plane_of in enumerate(planes):
                        to = pl.ds(pl.multiple_of((place // 4) * 256 + 128 * side, 128), 128)
                        w_down[place % 4, pl.ds(128 * group + 32 * field, 32), to] = plane_of

    from_other = {}

    def down(chunk, shift):
        place = column(shift)
        for pair in range(2):
            both = jnp.dot(
                turned[pl.ds(chunk * CR, CR), :], w_down[place, :, pl.ds(512 * pair, 512)],
                preferred_element_type=F32,
            ).astype(BF16)
            for z_at in range(2):
                for side in range(2):
                    lanes = slice(256 * z_at + 128 * side, 256 * z_at + 128 * side + 128)
                    part[chunk, side, place, 2 * pair + z_at] = both[:, lanes]
        from_other[chunk, shift] = remote(
            part.at[chunk, 1 - c, place], core_in.at[chunk, shift],
            c_send.at[chunk, shift], c_recv.at[chunk, shift], here(other),
        )

    top, bottom = pl.ds(0, HALF), pl.ds(HALF, HALF)

    def join(chunk, shift, rows):
        return part[chunk, c, column(shift), :, rows].astype(F32) + core_in[chunk, shift, :, rows].astype(F32)

    x_copies = {}

    def x_first(chunk):
        from_other[chunk, 2].wait_recv()
        sums[chunk, 2] = join(chunk, 2, pl.ds(0, CR)).astype(BF16)
        x_copies[chunk, "r1"] = remote(
            sums.at[chunk, 2, :, top], first_in.at[chunk, 0], x_send.at[chunk, 0], x_recv.at[chunk, 0], here(right)
        )
        x_copies[chunk, "l1"] = remote(
            sums.at[chunk, 2, :, bottom], first_in.at[chunk, 1], x_send.at[chunk, 1], x_recv.at[chunk, 1], here(left)
        )

    def x_second(chunk):
        from_other[chunk, 1].wait_recv()
        sums[chunk, 1, :, bottom] = join(chunk, 1, bottom).astype(BF16)
        x_copies[chunk, "r1"].wait_recv()
        sums[chunk, 1, :, top] = (join(chunk, 1, top) + first_in[chunk, 0].astype(F32)).astype(BF16)
        x_copies[chunk, "r2"] = remote(
            sums.at[chunk, 1], second_in.at[chunk, 0], y_send.at[chunk, 0], y_recv.at[chunk, 0], here(right)
        )
        from_other[chunk, 3].wait_recv()
        sums[chunk, 3, :, top] = join(chunk, 3, top).astype(BF16)
        x_copies[chunk, "l1"].wait_recv()
        sums[chunk, 3, :, bottom] = (join(chunk, 3, bottom) + first_in[chunk, 1].astype(F32)).astype(BF16)
        x_copies[chunk, "l2"] = remote(
            sums.at[chunk, 3], second_in.at[chunk, 1], y_send.at[chunk, 1], y_recv.at[chunk, 1], here(left)
        )

    z_copies = {}

    def z_first(chunk):
        from_other[chunk, 0].wait_recv()
        x_copies[chunk, "r2"].wait_recv()
        x_copies[chunk, "l2"].wait_recv()
        for near in (3, 2, 1, 0):
            to = z_of[near]
            value = (
                part[chunk, c, x, to].astype(F32) + core_in[chunk, 0, to].astype(F32)
                + second_in[chunk, 0, to].astype(F32) + second_in[chunk, 1, to].astype(F32)
            )
            mixed[chunk, near] = value.astype(BF16)
            if near:
                z_copies[chunk, near] = remote(
                    mixed.at[chunk, near], z_in.at[chunk, near], z_send.at[chunk, near], z_recv.at[chunk, near],
                    here(to * 8 + x * 2 + c),
                )

    def z_last(chunk):
        value = mixed[chunk, 0].astype(F32)
        for near in (1, 2, 3):
            z_copies[chunk, near].wait_recv()
            value = value + z_in[chunk, near].astype(F32)
        out_ref[pl.ds(chunk * CR, CR), :] = value.astype(BF16)

    send_own(0)
    from_z(0, 0)
    decode_piece(1)
    from_z(0, 1)
    from_x(0, 0)
    send_own(1)
    decode_piece(2)
    from_z(0, 2)
    from_x(0, 1)
    from_far(0, 0)
    decode_piece(3)
    from_z(0, 3)
    from_x(0, 2)
    from_far(0, 1)
    decode_piece(4)
    from_x(0, 3)
    from_far(0, 2)
    from_z(1, 0)
    decode_piece(5)
    from_far(0, 3)
    from_z(1, 1)
    decode_piece(6)
    from_z(1, 2)
    from_x(1, 0)
    decode_piece(7)
    from_z(1, 3)
    from_x(1, 1)
    from_core(0)
    gate_up(0, 0, 2)
    scatter(0, 0)
    from_x(1, 2)
    from_far(1, 0)
    gate_up(0, 2, 4)
    scatter(0, 1)
    from_x(1, 3)
    from_far(1, 1)
    gate_up(0, 4, 6)
    scatter(0, 2)
    from_far(1, 2)
    gate_up(0, 6, 7)
    scatter(0, 3)
    from_far(1, 3)
    from_core(1)
    for group in range(4):
        gate_up(1, 2 * group, min(2 * group + 2, TILES))
        scatter(1, group)
    rotate(0)
    spread_scales(down_scales, down_f32, 7)
    factor_load.wait()
    for tile in range(TILES):
        cols = pl.ds(128 * tile, 128)
        ordered[:, cols] = jnp.dot(factor[:, cols], order, preferred_element_type=F32).astype(BF16)
    down_load.wait()
    decode_down(0, 16)
    rotate(1)
    turn(0)
    down(0, 2)
    down(0, 1)
    x_first(0)
    down(0, 3)
    down(0, 0)
    x_second(0)
    turn(1)
    down(1, 2)
    down(1, 1)
    x_first(1)
    down(1, 3)
    down(1, 0)
    z_first(0)
    x_second(1)
    z_last(0)
    z_first(1)
    z_last(1)

    for copy in waiting:
        copy.wait_send()
    for group in range(4):
        for kept in range(2):
            @pl.when((c == group % 2) if kept else (c != group % 2))
            def _():
                sent = hidden.at[pl.ds(0, 16 - kept), :, group_cols[group]]
                pltpu.make_async_copy(sent, sent, a_send.at[group]).wait()
    for chunk in range(CHUNKS):
        for width in (256, 128):
            @pl.when((my_group(chunk) == 3) if width == 128 else (my_group(chunk) < 3))
            def _():
                sent = had_out.at[chunk, pl.ds(0, TP - 1), :, pl.ds(0, width)]
                pltpu.make_async_copy(sent, sent, b_send.at[chunk]).wait()


def shards(tokens, gate_codes, gate_scales, up_codes, up_scales, local_factor, down_codes, down_scales):
    vmem, hbm, dma = pl.BlockSpec(memory_space=pltpu.VMEM), pl.BlockSpec(memory_space=pl.ANY), pltpu.SemaphoreType.DMA
    return pl.pallas_call(
        kernel,
        out_shape=jax.ShapeDtypeStruct((ROWS, 128), BF16),
        in_specs=[vmem] * 4 + [hbm] * 4,
        out_specs=vmem,
        scratch_shapes=[
            pltpu.VMEM((1024, UNITS), jnp.int32),
            pltpu.VMEM((1024, UNITS), jnp.int32),
            pltpu.VMEM((224, 4096), jnp.int32),
            pltpu.VMEM((UNITS, UNITS), BF16),
            pltpu.VMEM((ROWS, 4096), BF16),
            pltpu.VMEM((TILES, 4096, 256), BF16),
            pltpu.VMEM((4, UNITS, 1024), BF16),
            pltpu.VMEM((UNITS, UNITS), BF16),
            pltpu.VMEM((32, 8, UNITS), F32),
            pltpu.VMEM((32, 8, UNITS), F32),
            pltpu.VMEM((7, 8, 4096), F32),
            pltpu.VMEM((16, 16, UNITS), BF16),
            pltpu.VMEM((2, TP, 16, 256), BF16),
            pltpu.VMEM((2, TP, 16, 256), BF16),
            pltpu.VMEM((16, 16, UNITS), BF16),
            pltpu.VMEM((ROWS, UNITS), BF16),
            pltpu.VMEM((CHUNKS, 2, 4, 4, CR, 128), BF16),
            pltpu.VMEM((CHUNKS, 4, 4, CR, 128), BF16),
            pltpu.VMEM((CHUNKS, 4, 4, CR, 128), BF16),
            pltpu.VMEM((CHUNKS, 2, 4, HALF, 128), BF16),
            pltpu.VMEM((CHUNKS, 2, 4, CR, 128), BF16),
            pltpu.VMEM((CHUNKS, 4, CR, 128), BF16),
            pltpu.VMEM((CHUNKS, 4, CR, 128), BF16),
            dma((10,)),
            dma((96,)),
            dma((CHUNKS, TP, 2)),
            dma((4,)),
            dma((CHUNKS,)),
            dma((CHUNKS,)),
            dma((CHUNKS,)),
            dma((CHUNKS, 4)),
            dma((CHUNKS, 4)),
            dma((CHUNKS, 2)),
            dma((CHUNKS, 2)),
            dma((CHUNKS, 2)),
            dma((CHUNKS, 2)),
            dma((CHUNKS, 4)),
            dma((CHUNKS, 4)),
        ],
        compiler_params=pltpu.CompilerParams(
            collective_id=0, has_side_effects=True, vmem_limit_bytes=58 * 1024 * 1024
        ),
        name="feed_forward",
    )(tokens, gate_scales, up_scales, down_scales, gate_codes, up_codes, local_factor, down_codes)


def solution(mesh):
    return jax.shard_map(
        shards,
        mesh=mesh,
        in_specs=(
            P("req", "tp"),
            P(None, "tp"),
            P(None, "tp"),
            P(None, "tp"),
            P(None, "tp"),
            P(),
            P("tp", None),
            P("tp", None),
        ),
        out_specs=P("req", "tp"),
        check_vma=False,
    )
```

time: 84.2 us -> 74.6 us (0.89)
  Pallas kernels: 81.9 us -> 73 us
    pallas_call x1, Pallas kernels: 81.9 us -> 73 us  [shards(): pl.pallas_call(kernel, out_shape=jax.ShapeDtypeStruct((ROWS, 128), BF16),...]
where the time goes in v5:
time: 74.6 us; the launch traced here: 74.5 us
  Pallas kernels  73 us (98%)
  local copies, waits for them, and re-layouts  1.47 us (2%)
    pallas_call x1, Pallas kernels, shards(): pl.pallas_call(kernel, out_shape=jax.ShapeDtypeStruct((ROWS, 128), BF16),...  73 us

profile of v5, /device:TPU:16, one launch (start us, length us, event | category | flops | bytes accessed | tf_op | source)
XLA Modules:
  0.0 74.5 jit_solution(423469012963826496)
XLA Ops:
  0.0 73.0 %feed_forward.1 = bf16[256,128]{1,0:T(8,128)(2,1)} custom-call(bf16[256,128]{1,0:T(8,128)(2,1)} %tok_in.1, bf16[32,896]{1,0:T(8,128)(2,1)} %gate_scales.1, bf16[32,896]{1,0:T(8,128)(2,1)} %up_scales.1, bf16[7,4096]{1,0:T(8,128)(2,1)} %down_scales.1, s32[1024,896]{1,0:T(8,128)} %gate_hbm.1, s32[1024,896]{1,0:T(8,128)} %up_hbm.1, bf16[896,896]{1,0:T(8,128)(2,1)} %factor_hbm.1, ...), custom_call_target="tpu_custom_call" | custom-call | tf_op jit(solution)/shard_map/feed_forward/pallas_call | solution.py:451
  73.0 1.5 %copy.10 = bf16[256,128]{1,0:T(8,128)(2,1)} copy(bf16[256,128]{1,0:T(8,128)(2,1)} %feed_forward.1) | data formatting | bytes 131072

commit v6 on v3

--- a/solution.py
+++ b/solution.py
@@ -151,11 +151,11 @@
         def _(side):
             group = (z_at * 4 + column(shift)) * 2 + side
             rows = pl.ds(pl.multiple_of(group * 32, 32), 32)
-            for tile in range(TILES):
-                cols = pl.ds(128 * tile, 128)
-                for place, codes, scales in ((0, gate_codes, gate_f32), (128, up_codes, up_f32)):
-                    planes = decode(codes[rows, cols], scales[group, :, cols])
-                    for field, plane in enumerate(planes):
+            for place, codes, scales in ((0, gate_codes, gate_f32), (128, up_codes, up_f32)):
+                words = [codes[rows, pl.ds(128 * tile, 128)] for tile in range(TILES)]
+                factors = [scales[group, :, pl.ds(128 * tile, 128)] for tile in range(TILES)]
+                for tile in range(TILES):
+                    for field, plane in enumerate(decode(words[tile], factors[tile])):
                         to = pl.ds(pl.multiple_of(z_at * 256 + side * 128 + 32 * field, 32), 32)
                         w_both[column(shift), tile, to, pl.ds(place, 128)] = plane
 
@@ -234,12 +234,13 @@
     def decode_down(first, stop):
         @pl.loop(first, stop)
         def _(place):
-            for group in range(TILES):
-                for side in range(2):
-                    cols = pl.ds(pl.multiple_of(place * 256 + 128 * side, 128), 128)
-                    planes = decode(down_codes[pl.ds(32 * group, 32), cols], down_f32[group, :, cols])
-                    for field, plane in enumerate(planes):
-                        to = pl.ds(pl.multiple_of((place // 4) * 256 + 128 * side, 128), 128)
+            for side in range(2):
+                cols = pl.ds(pl.multiple_of(place * 256 + 128 * side, 128), 128)
+                to = pl.ds(pl.multiple_of((place // 4) * 256 + 128 * side, 128), 128)
+                words = [down_codes[pl.ds(32 * group, 32), cols] for group in range(TILES)]
+                factors = [down_f32[group, :, cols] for group in range(TILES)]
+                for group in range(TILES):
+                    for field, plane in enumerate(decode(words[group], factors[group])):
                         w_down[place % 4, pl.ds(128 * group + 32 * field, 32), to] = plane
 
     from_other = {}

time: 73.1 us -> 73.2 us (level)
  no operation moved by 1% of the time
where the time goes in v6:
time: 73.2 us; the launch traced here: 73 us
  Pallas kernels  71.5 us (98%)
  local copies, waits for them, and re-layouts  1.47 us (2%)
    pallas_call x1, Pallas kernels, shards(): pl.pallas_call(kernel, out_shape=jax.ShapeDtypeStruct((ROWS, 128), BF16),...  71.5 us
    unnamed x1, local copies, waits for them, and re-layouts  1.47 us

profile of v6, /device:TPU:16, one launch (start us, length us, event | category | flops | bytes accessed | tf_op | source)
XLA Modules:
  0.0 73.0 jit_solution(9031460831712053410)
XLA Ops:
  0.0 71.5 %feed_forward.1 = bf16[256,128]{1,0:T(8,128)(2,1)} custom-call(bf16[256,128]{1,0:T(8,128)(2,1)} %tok_in.1, bf16[32,896]{1,0:T(8,128)(2,1)} %gate_scales.1, bf16[32,896]{1,0:T(8,128)(2,1)} %up_scales.1, bf16[7,4096]{1,0:T(8,128)(2,1)} %down_scales.1, s32[1024,896]{1,0:T(8,128)} %gate_hbm.1, s32[1024,896]{1,0:T(8,128)} %up_hbm.1, bf16[896,896]{1,0:T(8,128)(2,1)} %factor_hbm.1, ...), custom_call_target="tpu_custom_call" | custom-call | tf_op jit(solution)/shard_map/feed_forward/pallas_call | solution.py:426
  71.6 1.5 %copy.10 = bf16[256,128]{1,0:T(8,128)(2,1)} copy(bf16[256,128]{1,0:T(8,128)(2,1)} %feed_forward.1) | data formatting | bytes 131072

commit v7 on v6

--- a/solution.py
+++ b/solution.py
@@ -91,6 +91,11 @@
 
     pl.semaphore_wait(barrier, TP - 1)
 
+    def spread_scales(source, spread, groups):
+        scales = source[...].astype(F32)
+        for group in range(groups):
+            spread[group] = jnp.broadcast_to(scales[group : group + 1], spread.shape[1:])
+
     waiting = []
 
     def remote(src, dst, send, recv, device):
@@ -157,10 +162,12 @@
                 for tile in range(TILES):
                     for field, plane in enumerate(decode(words[tile], factors[tile])):
                         to = pl.ds(pl.multiple_of(z_at * 256 + side * 128 + 32 * field, 32), 32)
-                        w_both[column(shift), tile, to, pl.ds(place, 128)] = plane
-
-    def product(shift, tile):
-        return jnp.dot(tok[column(shift)], w_both[column(shift), tile], preferred_element_type=F32)
+                        w_both[column(shift), to, pl.ds(256 * tile + place, 128)] = plane
+
+    both_cols = [pl.ds(0, 512), pl.ds(512, 512), pl.ds(1024, 512), pl.ds(1536, 256)]
+
+    def product(shift, group):
+        return jnp.dot(tok[column(shift)], w_both[column(shift), :, both_cols[group]], preferred_element_type=F32)
 
     chip = me // 2
     wide, narrow = pl.ds(0, 256), pl.ds(0, 128)
@@ -323,10 +330,8 @@
         out_ref[pl.ds(chunk * CR, CR), :] = total.astype(BF16)
 
     from_z(0)
-    for source, spread, groups in ((gate_scales, gate_f32, 32), (up_scales, up_f32, 32), (down_scales, down_f32, 7)):
-        scales = source[...].astype(F32)
-        for group in range(groups):
-            spread[group] = jnp.broadcast_to(scales[group : group + 1], spread.shape[1:])
+    spread_scales(gate_scales, gate_f32, 32)
+    spread_scales(up_scales, up_f32, 32)
     for z_at in range(4):
         decode_piece(0, z_at)
     from_z(1)
@@ -349,36 +354,34 @@
     from_far(2)
     from_core(0)
 
-    @pl.loop(0, TILES)
-    def _(tile):
-        total[tile] = product(0, tile)
+    for group in range(4):
+        total[:, both_cols[group]] = product(0, group)
 
     from_far(3)
     for z_at in range(4):
         decode_piece(2, z_at)
+    from_core(1)
+    from_core(3)
+
+    for group in range(4):
+        total[:, both_cols[group]] += product(1, group) + product(3, group)
+
+    from_core(2)
+    for group in range(4):
+        both = total[:, both_cols[group]] + product(2, group)
+        for tile in range(2 * group, min(2 * group + 2, TILES)):
+            start = 256 * (tile - 2 * group)
+            gate, up = both[:, start : start + 128], both[:, start + 128 : start + 256]
+            value = gate / (1.0 + jnp.exp(-gate)) * up
+            hidden[:, :, pl.ds(128 * tile, 128)] = value.astype(BF16).reshape(16, 16, 128)
+
+        scatter(group)
+
     factor_load.wait()
     for tile in range(TILES):
         cols = pl.ds(128 * tile, 128)
         ordered[:, cols] = jnp.dot(factor[:, cols], order, preferred_element_type=F32).astype(BF16)
-    from_core(1)
-    from_core(3)
-
-    @pl.loop(0, TILES)
-    def _(tile):
-        total[tile] += product(1, tile) + product(3, tile)
-
-    from_core(2)
-    for group in range(4):
-        @pl.loop(2 * group, min(2 * group + 2, TILES))
-        def _(tile):
-            both = total[tile] + product(2, tile)
-            gate, up = both[:, :128], both[:, 128:]
-            value = gate / (1.0 + jnp.exp(-gate)) * up
-            lanes = pl.ds(pl.multiple_of(tile * 128, 128), 128)
-            hidden[:, :, lanes] = value.astype(BF16).reshape(16, 16, 128)
-
-        scatter(group)
-
+    spread_scales(down_scales, down_f32, 7)
     down_load.wait()
     decode_down(0, 8)
     rotate_turn(0)
@@ -434,13 +437,13 @@
             pltpu.VMEM((224, 4096), jnp.int32),
             pltpu.VMEM((UNITS, UNITS), BF16),
             pltpu.VMEM((4, ROWS, 1024), BF16),
-            pltpu.VMEM((4, TILES, 1024, 256), BF16),
+            pltpu.VMEM((4, 1024, 2 * UNITS), BF16),
             pltpu.VMEM((4, UNITS, 1024), BF16),
             pltpu.VMEM((UNITS, UNITS), BF16),
             pltpu.VMEM((32, 8, UNITS), F32),
             pltpu.VMEM((32, 8, UNITS), F32),
             pltpu.VMEM((7, 8, 4096), F32),
-            pltpu.VMEM((TILES, ROWS, 256), F32),
+            pltpu.VMEM((ROWS, 2 * UNITS), F32),
             pltpu.VMEM((16, 16, UNITS), BF16),
             pltpu.VMEM((2, TP, 16, 256), BF16),
             pltpu.VMEM((2, TP, 16, 256), BF16),

time: 73.2 us -> 71.6 us (0.978)
  Pallas kernels: 71.5 us -> 69.9 us
    pallas_call x1, Pallas kernels: 71.5 us -> 69.9 us  [shards(): pl.pallas_call(kernel, out_shape=jax.ShapeDtypeStruct((ROWS, 128), BF16),...]
where the time goes in v7:
time: 71.6 us; the launch traced here: 71.4 us
  Pallas kernels  69.9 us (98%)
  local copies, waits for them, and re-layouts  1.47 us (2%)
    pallas_call x1, Pallas kernels, shards(): pl.pallas_call(kernel, out_shape=jax.ShapeDtypeStruct((ROWS, 128), BF16),...  69.9 us
    unnamed x1, local copies, waits for them, and re-layouts  1.47 us

profile of v7, /device:TPU:16, one launch (start us, length us, event | category | flops | bytes accessed | tf_op | source)
XLA Modules:
  0.0 71.4 jit_solution(3694975781784337253)
XLA Ops:
  0.0 69.9 %feed_forward.1 = bf16[256,128]{1,0:T(8,128)(2,1)} custom-call(bf16[256,128]{1,0:T(8,128)(2,1)} %tok_in.1, bf16[32,896]{1,0:T(8,128)(2,1)} %gate_scales.1, bf16[32,896]{1,0:T(8,128)(2,1)} %up_scales.1, bf16[7,4096]{1,0:T(8,128)(2,1)} %down_scales.1, s32[1024,896]{1,0:T(8,128)} %gate_hbm.1, s32[1024,896]{1,0:T(8,128)} %up_hbm.1, bf16[896,896]{1,0:T(8,128)(2,1)} %factor_hbm.1, ...), custom_call_target="tpu_custom_call" | custom-call | tf_op jit(solution)/shard_map/feed_forward/pallas_call | solution.py:429
  69.9 1.5 %copy.10 = bf16[256,128]{1,0:T(8,128)(2,1)} copy(bf16[256,128]{1,0:T(8,128)(2,1)} %feed_forward.1) | data formatting | bytes 131072

commit v8 on v7

--- a/solution.py
+++ b/solution.py
@@ -15,7 +15,6 @@
 TILES = 7
 CHUNKS = 2
 CR = ROWS // CHUNKS
-HALF = CR // 2
 F32 = jnp.float32
 BF16 = jnp.bfloat16
 
@@ -42,15 +41,15 @@
 def kernel(
     tok_in, gate_scales, up_scales, down_scales, gate_hbm, up_hbm, factor_hbm, down_hbm, out_ref,
     gate_codes, up_codes, down_codes, factor, tok, w_both, w_down, ordered, gate_f32, up_f32, down_f32, total,
-    hidden, had_in, had_out, rotated, turned, part, core_in, sums, first_in, second_in, mixed, z_in,
-    load_sem, tok_send, tok_recv, a_send, a_recv, b_send, b_recv, c_send, c_recv, x_send, x_recv,
-    y_send, y_recv, z_send, z_recv,
+    hidden, had_in, had_out, rotated, turned, part, core_in, sums, x_in, mixed, z_in,
+    load_sem, tok_send, tok_recv, a_send, a_recv, b_send, b_recv, c_send, c_recv, x_send, x_recv, z_send, z_recv,
 ):
     me = lax.axis_index("tp")
     z, x, c = me // 8, (me // 2) % 4, me % 2
     other = me + 1 - 2 * c
     right = z * 8 + ((x + 1) % 4) * 2 + c
     left = z * 8 + ((x + 3) % 4) * 2 + c
+    far = z * 8 + ((x + 2) % 4) * 2 + c
     z_of = [z, z + 1 - 2 * (z % 2), (z + 2) % 4, 3 - z]
 
     barrier = pltpu.get_barrier_semaphore()
@@ -107,13 +106,13 @@
         waiting.append(copy)
         return copy
 
-    def pass_on(block, device, row=0, count=ROWS):
-        where = tokens_of(block, row, count)
-        remote(where, where, tok_send.at[len(waiting)], tok_recv.at[block, 1 if row else 0], device)
-
-    def arrived(block, row=0, count=ROWS):
-        where = tokens_of(block, row, count)
-        pltpu.make_async_copy(where, where, tok_recv.at[block, 1 if row else 0]).wait()
+    def pass_on(block, device):
+        where = tokens_of(block, 0, ROWS)
+        remote(where, where, tok_send.at[len(waiting)], tok_recv.at[block], device)
+
+    def arrived(block):
+        where = tokens_of(block, 0, ROWS)
+        pltpu.make_async_copy(where, where, tok_recv.at[block]).wait()
 
     def at(near, shift):
         return z_of[near] * 8 + column(shift) * 2 + c
@@ -121,28 +120,20 @@
     def from_z(near):
         if near:
             arrived(at(near, 0))
-        pass_on(at(near, 0), right)
-        pass_on(at(near, 0), left)
-        if not near:
+        else:
             for peer in (1, 2, 3):
                 pass_on(me, at(peer, 0))
-        pass_on(at(near, 0), other)
+        for device in (right, left, far, other):
+            pass_on(at(near, 0), device)
 
     def from_x(near):
-        block = at(near, 3)
-        arrived(block)
-        pass_on(block, right, 0, ROWS // 2)
-        pass_on(block, other)
-        block = at(near, 1)
-        arrived(block)
-        pass_on(block, left, ROWS // 2, ROWS // 2)
-        pass_on(block, other)
+        for shift in (3, 1):
+            arrived(at(near, shift))
+            pass_on(at(near, shift), other)
 
     def from_far(near):
-        block = at(near, 2)
-        arrived(block, 0, ROWS // 2)
-        arrived(block, ROWS // 2, ROWS // 2)
-        pass_on(block, other)
+        arrived(at(near, 2))
+        pass_on(at(near, 2), other)
 
     def from_core(shift):
         for z_at in range(4):
@@ -270,50 +261,27 @@
                 c_send.at[chunk, shift], c_recv.at[chunk, shift], other,
             )
 
-    top, bottom = pl.ds(0, HALF), pl.ds(HALF, HALF)
-
-    def join(chunk, shift, rows):
-        return part[chunk, c, column(shift), :, rows].astype(F32) + core_in[chunk, shift, :, rows].astype(F32)
-
     x_copies = {}
 
-    def x_first(chunk):
-        from_other[chunk, 2].wait_recv()
-        sums[chunk, 2] = join(chunk, 2, pl.ds(0, CR)).astype(BF16)
-        x_copies[chunk, "r1"] = remote(
-            sums.at[chunk, 2, :, top], first_in.at[chunk, 0], x_send.at[chunk, 0], x_recv.at[chunk, 0], right
-        )
-        x_copies[chunk, "l1"] = remote(
-            sums.at[chunk, 2, :, bottom], first_in.at[chunk, 1], x_send.at[chunk, 1], x_recv.at[chunk, 1], left
-        )
-
-    def x_second(chunk):
-        from_other[chunk, 1].wait_recv()
-        sums[chunk, 1, :, bottom] = join(chunk, 1, bottom).astype(BF16)
-        x_copies[chunk, "r1"].wait_recv()
-        sums[chunk, 1, :, top] = (join(chunk, 1, top) + first_in[chunk, 0].astype(F32)).astype(BF16)
-        x_copies[chunk, "r2"] = remote(
-            sums.at[chunk, 1], second_in.at[chunk, 0], y_send.at[chunk, 0], y_recv.at[chunk, 0], right
-        )
-        from_other[chunk, 3].wait_recv()
-        sums[chunk, 3, :, top] = join(chunk, 3, top).astype(BF16)
-        x_copies[chunk, "l1"].wait_recv()
-        sums[chunk, 3, :, bottom] = (join(chunk, 3, bottom) + first_in[chunk, 1].astype(F32)).astype(BF16)
-        x_copies[chunk, "l2"] = remote(
-            sums.at[chunk, 3], second_in.at[chunk, 1], y_send.at[chunk, 1], y_recv.at[chunk, 1], left
+    def to_x(chunk, shift, device):
+        from_other[chunk, shift].wait_recv()
+        value = part[chunk, c, column(shift)].astype(F32) + core_in[chunk, shift].astype(F32)
+        sums[chunk, shift] = value.astype(BF16)
+        x_copies[chunk, shift] = remote(
+            sums.at[chunk, shift], x_in.at[chunk, shift], x_send.at[chunk, shift], x_recv.at[chunk, shift], device
         )
 
     z_copies = {}
 
     def z_first(chunk):
         from_other[chunk, 0].wait_recv()
-        x_copies[chunk, "r2"].wait_recv()
-        x_copies[chunk, "l2"].wait_recv()
+        for shift in (1, 3, 2):
+            x_copies[chunk, shift].wait_recv()
         for near in (3, 2, 1, 0):
             to = z_of[near]
             value = (
                 part[chunk, c, x, to].astype(F32) + core_in[chunk, 0, to].astype(F32)
-                + second_in[chunk, 0, to].astype(F32) + second_in[chunk, 1, to].astype(F32)
+                + x_in[chunk, 1, to].astype(F32) + x_in[chunk, 2, to].astype(F32) + x_in[chunk, 3, to].astype(F32)
             )
             mixed[chunk, near] = value.astype(BF16)
             if near:
@@ -400,12 +368,14 @@
     turned[...] = (whole * math.sqrt(TP)).astype(BF16)
     down(2)
     down(1)
-    x_first(0)
-    x_first(1)
+    for chunk in range(CHUNKS):
+        to_x(chunk, 2, far)
     down(3)
+    for chunk in range(CHUNKS):
+        to_x(chunk, 1, right)
     down(0)
-    x_second(0)
-    x_second(1)
+    for chunk in range(CHUNKS):
+        to_x(chunk, 3, left)
     z_first(0)
     z_first(1)
     z_last(0)
@@ -452,23 +422,20 @@
             pltpu.VMEM((CHUNKS, 2, 4, 4, CR, 128), BF16),
             pltpu.VMEM((CHUNKS, 4, 4, CR, 128), BF16),
             pltpu.VMEM((CHUNKS, 4, 4, CR, 128), BF16),
-            pltpu.VMEM((CHUNKS, 2, 4, HALF, 128), BF16),
-            pltpu.VMEM((CHUNKS, 2, 4, CR, 128), BF16),
+            pltpu.VMEM((CHUNKS, 4, 4, CR, 128), BF16),
             pltpu.VMEM((CHUNKS, 4, CR, 128), BF16),
             pltpu.VMEM((CHUNKS, 4, CR, 128), BF16),
             dma((34,)),
             dma((48,)),
-            dma((TP, 2)),
+            dma((TP,)),
             dma((4,)),
             dma((2,)),
             dma((2,)),
             dma((4,)),
             dma((CHUNKS, 4)),
             dma((CHUNKS, 4)),
-            dma((CHUNKS, 2)),
-            dma((CHUNKS, 2)),
-            dma((CHUNKS, 2)),
-            dma((CHUNKS, 2)),
+            dma((CHUNKS, 4)),
+            dma((CHUNKS, 4)),
             dma((CHUNKS, 4)),
             dma((CHUNKS, 4)),
         ],

time: 71.6 us -> 73.7 us (1.029)
  Pallas kernels: 69.9 us -> 72 us
    pallas_call x1, Pallas kernels: 69.9 us -> 72 us  [shards(): pl.pallas_call(kernel, out_shape=jax.ShapeDtypeStruct((ROWS, 128), BF16),...]
where the time goes in v8:
time: 73.7 us; the launch traced here: 73.5 us
  Pallas kernels  72 us (98%)
  local copies, waits for them, and re-layouts  1.47 us (2%)
    pallas_call x1, Pallas kernels, shards(): pl.pallas_call(kernel, out_shape=jax.ShapeDtypeStruct((ROWS, 128), BF16),...  72 us

profile of v8, /device:TPU:16, one launch (start us, length us, event | category | flops | bytes accessed | tf_op | source)
XLA Modules:
  0.0 73.5 jit_solution(17015623194661806668)
XLA Ops:
  0.0 72.0 %feed_forward.1 = bf16[256,128]{1,0:T(8,128)(2,1)} custom-call(bf16[256,128]{1,0:T(8,128)(2,1)} %tok_in.1, bf16[32,896]{1,0:T(8,128)(2,1)} %gate_scales.1, bf16[32,896]{1,0:T(8,128)(2,1)} %up_scales.1, bf16[7,4096]{1,0:T(8,128)(2,1)} %down_scales.1, s32[1024,896]{1,0:T(8,128)} %gate_hbm.1, s32[1024,896]{1,0:T(8,128)} %up_hbm.1, bf16[896,896]{1,0:T(8,128)(2,1)} %factor_hbm.1, ...), custom_call_target="tpu_custom_call" | custom-call | tf_op jit(solution)/shard_map/feed_forward/pallas_call | solution.py:399
  72.0 1.5 %copy.10 = bf16[256,128]{1,0:T(8,128)(2,1)} copy(bf16[256,128]{1,0:T(8,128)(2,1)} %feed_forward.1) | data formatting | bytes 131072

commit v9 on v7

--- a/solution.py
+++ b/solution.py
@@ -13,7 +13,7 @@
 ROWS = 256
 UNITS = 896
 TILES = 7
-CHUNKS = 2
+CHUNKS = 4
 CR = ROWS // CHUNKS
 HALF = CR // 2
 F32 = jnp.float32
@@ -89,64 +89,10 @@
 
     tokens_of(me, 0, ROWS)[...] = jnp.dot(tok_in[...], order, preferred_element_type=F32).astype(BF16)
 
-    pl.semaphore_wait(barrier, TP - 1)
-
     def spread_scales(source, spread, groups):
         scales = source[...].astype(F32)
         for group in range(groups):
             spread[group] = jnp.broadcast_to(scales[group : group + 1], spread.shape[1:])
-
-    waiting = []
-
-    def remote(src, dst, send, recv, device):
-        copy = pltpu.make_async_remote_copy(
-            src_ref=src, dst_ref=dst, send_sem=send, recv_sem=recv,
-            device_id={"tp": device}, device_id_type=MESH,
-        )
-        copy.start()
-        waiting.append(copy)
-        return copy
-
-    def pass_on(block, device, row=0, count=ROWS):
-        where = tokens_of(block, row, count)
-        remote(where, where, tok_send.at[len(waiting)], tok_recv.at[block, 1 if row else 0], device)
-
-    def arrived(block, row=0, count=ROWS):
-        where = tokens_of(block, row, count)
-        pltpu.make_async_copy(where, where, tok_recv.at[block, 1 if row else 0]).wait()
-
-    def at(near, shift):
-        return z_of[near] * 8 + column(shift) * 2 + c
-
-    def from_z(near):
-        if near:
-            arrived(at(near, 0))
-        pass_on(at(near, 0), right)
-        pass_on(at(near, 0), left)
-        if not near:
-            for peer in (1, 2, 3):
-                pass_on(me, at(peer, 0))
-        pass_on(at(near, 0), other)
-
-    def from_x(near):
-        block = at(near, 3)
-        arrived(block)
-        pass_on(block, right, 0, ROWS // 2)
-        pass_on(block, other)
-        block = at(near, 1)
-        arrived(block)
-        pass_on(block, left, ROWS // 2, ROWS // 2)
-        pass_on(block, other)
-
-    def from_far(near):
-        block = at(near, 2)
-        arrived(block, 0, ROWS // 2)
-        arrived(block, ROWS // 2, ROWS // 2)
-        pass_on(block, other)
-
-    def from_core(shift):
-        for z_at in range(4):
-            arrived(z_at * 8 + column(shift) * 2 + 1 - c)
 
     def decode_piece(shift, z_at):
         for copy in loads[shift, z_at]:
@@ -163,6 +109,64 @@
                     for field, plane in enumerate(decode(words[tile], factors[tile])):
                         to = pl.ds(pl.multiple_of(z_at * 256 + side * 128 + 32 * field, 32), 32)
                         w_both[column(shift), to, pl.ds(256 * tile + place, 128)] = plane
+
+    spread_scales(gate_scales, gate_f32, 32)
+    spread_scales(up_scales, up_f32, 32)
+    decode_piece(0, 0)
+
+    pl.semaphore_wait(barrier, TP - 1)
+
+    waiting = []
+
+    def remote(src, dst, send, recv, device):
+        copy = pltpu.make_async_remote_copy(
+            src_ref=src, dst_ref=dst, send_sem=send, recv_sem=recv,
+            device_id={"tp": device}, device_id_type=MESH,
+        )
+        copy.start()
+        waiting.append(copy)
+        return copy
+
+    def pass_on(block, device, row=0, count=ROWS):
+        where = tokens_of(block, row, count)
+        remote(where, where, tok_send.at[len(waiting)], tok_recv.at[block, 1 if row else 0], device)
+
+    def arrived(block, row=0, count=ROWS):
+        where = tokens_of(block, row, count)
+        pltpu.make_async_copy(where, where, tok_recv.at[block, 1 if row else 0]).wait()
+
+    def at(near, shift):
+        return z_of[near] * 8 + column(shift) * 2 + c
+
+    def from_z(near):
+        if near:
+            arrived(at(near, 0))
+        pass_on(at(near, 0), right)
+        pass_on(at(near, 0), left)
+        if not near:
+            for peer in (1, 2, 3):
+                pass_on(me, at(peer, 0))
+        pass_on(at(near, 0), other)
+
+    def from_x(near):
+        block = at(near, 3)
+        arrived(block)
+        pass_on(block, right, 0, ROWS // 2)
+        pass_on(block, other)
+        block = at(near, 1)
+        arrived(block)
+        pass_on(block, left, ROWS // 2, ROWS // 2)
+        pass_on(block, other)
+
+    def from_far(near):
+        block = at(near, 2)
+        arrived(block, 0, ROWS // 2)
+        arrived(block, ROWS // 2, ROWS // 2)
+        pass_on(block, other)
+
+    def from_core(shift):
+        for z_at in range(4):
+            arrived(z_at * 8 + column(shift) * 2 + 1 - c)
 
     both_cols = [pl.ds(0, 512), pl.ds(512, 512), pl.ds(1024, 512), pl.ds(1536, 256)]
 
@@ -330,9 +334,7 @@
         out_ref[pl.ds(chunk * CR, CR), :] = total.astype(BF16)
 
     from_z(0)
-    spread_scales(gate_scales, gate_f32, 32)
-    spread_scales(up_scales, up_f32, 32)
-    for z_at in range(4):
+    for z_at in range(1, 4):
         decode_piece(0, z_at)
     from_z(1)
     from_x(0)
@@ -357,15 +359,15 @@
     for group in range(4):
         total[:, both_cols[group]] = product(0, group)
 
-    from_far(3)
     for z_at in range(4):
         decode_piece(2, z_at)
     from_core(1)
+    for group in range(4):
+        total[:, both_cols[group]] += product(1, group)
+    from_far(3)
     from_core(3)
-
     for group in range(4):
-        total[:, both_cols[group]] += product(1, group) + product(3, group)
-
+        total[:, both_cols[group]] += product(3, group)
     from_core(2)
     for group in range(4):
         both = total[:, both_cols[group]] + product(2, group)
@@ -400,16 +402,16 @@
     turned[...] = (whole * math.sqrt(TP)).astype(BF16)
     down(2)
     down(1)
-    x_first(0)
-    x_first(1)
+    for chunk in range(CHUNKS):
+        x_first(chunk)
     down(3)
     down(0)
-    x_second(0)
-    x_second(1)
-    z_first(0)
-    z_first(1)
-    z_last(0)
-    z_last(1)
+    for chunk in range(CHUNKS):
+        x_second(chunk)
+    for chunk in range(CHUNKS):
+        z_first(chunk)
+    for chunk in range(CHUNKS):
+        z_last(chunk)
 
     for copy in waiting:
         copy.wait_send()

time: 71.6 us -> 71.6 us (level)
  no operation moved by 1% of the time
where the time goes in v9:
time: 71.6 us; the launch traced here: 71.4 us
  Pallas kernels  69.9 us (98%)
  local copies, waits for them, and re-layouts  1.47 us (2%)
    pallas_call x1, Pallas kernels, shards(): pl.pallas_call(kernel, out_shape=jax.ShapeDtypeStruct((ROWS, 128), BF16),...  69.9 us
    unnamed x1, local copies, waits for them, and re-layouts  1.47 us

profile of v9, /device:TPU:16, one launch (start us, length us, event | category | flops | bytes accessed | tf_op | source)
XLA Modules:
  0.0 71.4 jit_solution(3888623565085904030)
XLA Ops:
  0.0 69.9 %feed_forward.1 = bf16[256,128]{1,0:T(8,128)(2,1)} custom-call(bf16[256,128]{1,0:T(8,128)(2,1)} %tok_in.1, bf16[32,896]{1,0:T(8,128)(2,1)} %gate_scales.1, bf16[32,896]{1,0:T(8,128)(2,1)} %up_scales.1, bf16[7,4096]{1,0:T(8,128)(2,1)} %down_scales.1, s32[1024,896]{1,0:T(8,128)} %gate_hbm.1, s32[1024,896]{1,0:T(8,128)} %up_hbm.1, bf16[896,896]{1,0:T(8,128)(2,1)} %factor_hbm.1, ...), custom_call_target="tpu_custom_call" | custom-call | tf_op jit(solution)/shard_map/feed_forward/pallas_call | solution.py:431
  69.9 1.5 %copy.10 = bf16[256,128]{1,0:T(8,128)(2,1)} copy(bf16[256,128]{1,0:T(8,128)(2,1)} %feed_forward.1) | data formatting | bytes 131072

commit v10 on v7

--- a/solution.py
+++ b/solution.py
@@ -98,10 +98,12 @@
 
     waiting = []
 
+    def here(device):
+        return {"tp": device}
+
     def remote(src, dst, send, recv, device):
         copy = pltpu.make_async_remote_copy(
-            src_ref=src, dst_ref=dst, send_sem=send, recv_sem=recv,
-            device_id={"tp": device}, device_id_type=MESH,
+            src_ref=src, dst_ref=dst, send_sem=send, recv_sem=recv, device_id=device, device_id_type=MESH,
         )
         copy.start()
         waiting.append(copy)
@@ -109,7 +111,7 @@
 
     def pass_on(block, device, row=0, count=ROWS):
         where = tokens_of(block, row, count)
-        remote(where, where, tok_send.at[len(waiting)], tok_recv.at[block, 1 if row else 0], device)
+        remote(where, where, tok_send.at[len(waiting)], tok_recv.at[block, 1 if row else 0], here(device))
 
     def arrived(block, row=0, count=ROWS):
         where = tokens_of(block, row, count)
@@ -166,45 +168,55 @@
 
     both_cols = [pl.ds(0, 512), pl.ds(512, 512), pl.ds(1024, 512), pl.ds(1536, 256)]
 
-    def product(shift, group):
-        return jnp.dot(tok[column(shift)], w_both[column(shift), :, both_cols[group]], preferred_element_type=F32)
-
-    chip = me // 2
-    wide, narrow = pl.ds(0, 256), pl.ds(0, 128)
+    def product(shift, group, rows=pl.ds(0, ROWS)):
+        return jnp.dot(
+            tok[column(shift), rows, :], w_both[column(shift), :, both_cols[group]], preferred_element_type=F32
+        )
+
     group_cols = [pl.ds(0, 256), pl.ds(256, 256), pl.ds(512, 256), pl.ds(768, 128)]
     group_width = [256, 256, 256, 128]
 
-    def scatter(group):
+    row_tile = z * 2 + x // 2
+
+    def scatter(chunk, group):
         side, lanes = group % 2, pl.ds(0, group_width[group])
-
-        def give(to_chip):
+        parity = (group // 2 + chunk) % 2
+
+        def give(step):
+            dz, half = (z + 1 + step // 2) % 4, (x // 2 + step) % 2
+            device, tile = dz * 8 + (parity + 2 * half) * 2 + side, chunk * 8 + dz * 2 + half
             pltpu.make_async_remote_copy(
-                src_ref=hidden.at[to_chip, :, group_cols[group]], dst_ref=had_in.at[group // 2, me, :, lanes],
-                send_sem=a_send.at[group], recv_sem=a_recv.at[group // 2],
-                device_id={"tp": to_chip * 2 + side}, device_id_type=MESH,
+                src_ref=hidden.at[tile, :, group_cols[group]], dst_ref=had_in.at[chunk, me, :, lanes],
+                send_sem=a_send.at[group], recv_sem=a_recv.at[chunk],
+                device_id=here(device), device_id_type=MESH,
             ).start()
 
-        @pl.loop(1, 16)
-        def _(step):
-            give((chip + 1 + (step + 2) % 15) % 16)
-
-        @pl.when(c == side)
+        for step in range(6):
+            give(step)
+        give(7)
+        own = jnp.logical_and(c == side, x % 2 == parity)
+
+        @pl.when(own)
         def _():
             pltpu.make_async_copy(
-                hidden.at[chip, :, group_cols[group]], had_in.at[group // 2, me, :, lanes], a_recv.at[group // 2]
+                hidden.at[chunk * 8 + row_tile, :, group_cols[group]], had_in.at[chunk, me, :, lanes],
+                a_recv.at[chunk],
             ).start()
 
-        @pl.when(c != side)
+        @pl.when(jnp.logical_not(own))
         def _():
-            give(chip)
-
-    def rotate(group):
-        turn, lanes = group // 2, pl.ds(0, group_width[group])
-        everything = had_in.at[turn, :, :, lanes]
-        pltpu.make_async_copy(everything, everything, a_recv.at[turn]).wait()
-        for tile in range(group_width[group] // 128):
+            give(6)
+
+    def my_group(chunk):
+        return 2 * ((x + chunk) % 2) + c
+
+    def rotate_part(chunk, width, to_cols):
+        lanes = pl.ds(0, width)
+        everything = had_in.at[chunk, :, :, lanes]
+        pltpu.make_async_copy(everything, everything, a_recv.at[chunk]).wait()
+        for tile in range(width // 128):
             cols = pl.ds(128 * tile, 128)
-            held = [had_in[turn, source, :, cols].astype(F32) * (1.0 / TP) for source in range(TP)]
+            held = [had_in[chunk, source, :, cols].astype(F32) * (1.0 / TP) for source in range(TP)]
             apart = 1
             while apart < TP:
                 held = [
@@ -213,30 +225,38 @@
                 ]
                 apart *= 2
             for target in range(TP):
-                had_out[turn, target, :, cols] = held[target].astype(BF16)
+                had_out[chunk, target, :, cols] = held[target].astype(BF16)
 
         @pl.loop(1, TP)
         def _(step):
             device = (me + 1 + (step + 6) % (TP - 1)) % TP
             pltpu.make_async_remote_copy(
-                src_ref=had_out.at[turn, device, :, lanes], dst_ref=rotated.at[chip, :, group_cols[group]],
-                send_sem=b_send.at[turn], recv_sem=b_recv.at[group],
-                device_id={"tp": device}, device_id_type=MESH,
+                src_ref=had_out.at[chunk, device, :, lanes], dst_ref=rotated.at[chunk * 8 + row_tile, :, to_cols],
+                send_sem=b_send.at[chunk], recv_sem=b_recv.at[chunk],
+                device_id=here(device), device_id_type=MESH,
             ).start()
 
         pltpu.make_async_copy(
-            had_out.at[turn, me, :, lanes], rotated.at[chip, :, group_cols[group]], b_recv.at[group]
+            had_out.at[chunk, me, :, lanes], rotated.at[chunk * 8 + row_tile, :, to_cols], b_recv.at[chunk]
         ).start()
 
-    def rotate_turn(turn):
-        for side in range(2):
-            @pl.when(c == side)
-            def _():
-                rotate(2 * turn + side)
-
-    def back(group):
-        everything = rotated.at[:, :, group_cols[group]]
-        pltpu.make_async_copy(everything, everything, b_recv.at[group]).wait()
+    def rotate(chunk):
+        group = my_group(chunk)
+
+        @pl.when(group < 3)
+        def _():
+            rotate_part(chunk, 256, pl.ds(pl.multiple_of(group * 256, 256), 256))
+
+        @pl.when(group == 3)
+        def _():
+            rotate_part(chunk, 128, group_cols[3])
+
+    def turn(chunk):
+        tiles = pl.ds(8 * chunk, 8)
+        everything = rotated.at[tiles]
+        pltpu.make_async_copy(everything, everything, b_recv.at[chunk]).wait()
+        value = jnp.dot(rotated[tiles].reshape(CR, UNITS), ordered[...], preferred_element_type=F32)
+        turned[pl.ds(chunk * CR, CR), :] = (value * math.sqrt(TP)).astype(BF16)
 
     def decode_down(first, stop):
         @pl.loop(first, stop)
@@ -252,23 +272,21 @@
 
     from_other = {}
 
-    def down(shift):
+    def down(chunk, shift):
         place = column(shift)
         for pair in range(2):
             both = jnp.dot(
-                turned[...], w_down[place, :, pl.ds(512 * pair, 512)], preferred_element_type=F32
+                turned[pl.ds(chunk * CR, CR), :], w_down[place, :, pl.ds(512 * pair, 512)],
+                preferred_element_type=F32,
             ).astype(BF16)
-            for chunk in range(CHUNKS):
-                rows = slice(chunk * CR, (chunk + 1) * CR)
-                for z_at in range(2):
-                    for side in range(2):
-                        lanes = slice(256 * z_at + 128 * side, 256 * z_at + 128 * side + 128)
-                        part[chunk, side, place, 2 * pair + z_at] = both[rows, lanes]
-        for chunk in range(CHUNKS):
-            from_other[chunk, shift] = remote(
-                part.at[chunk, 1 - c, place], core_in.at[chunk, shift],
-                c_send.at[chunk, shift], c_recv.at[chunk, shift], other,
-            )
+            for z_at in range(2):
+                for side in range(2):
+                    lanes = slice(256 * z_at + 128 * side, 256 * z_at + 128 * side + 128)
+                    part[chunk, side, place, 2 * pair + z_at] = both[:, lanes]
+        from_other[chunk, shift] = remote(
+            part.at[chunk, 1 - c, place], core_in.at[chunk, shift],
+            c_send.at[chunk, shift], c_recv.at[chunk, shift], here(other),
+        )
 
     top, bottom = pl.ds(0, HALF), pl.ds(HALF, HALF)
 
@@ -281,10 +299,10 @@
         from_other[chunk, 2].wait_recv()
         sums[chunk, 2] = join(chunk, 2, pl.ds(0, CR)).astype(BF16)
         x_copies[chunk, "r1"] = remote(
-            sums.at[chunk, 2, :, top], first_in.at[chunk, 0], x_send.at[chunk, 0], x_recv.at[chunk, 0], right
+            sums.at[chunk, 2, :, top], first_in.at[chunk, 0], x_send.at[chunk, 0], x_recv.at[chunk, 0], here(right)
         )
         x_copies[chunk, "l1"] = remote(
-            sums.at[chunk, 2, :, bottom], first_in.at[chunk, 1], x_send.at[chunk, 1], x_recv.at[chunk, 1], left
+            sums.at[chunk, 2, :, bottom], first_in.at[chunk, 1], x_send.at[chunk, 1], x_recv.at[chunk, 1], here(left)
         )
 
     def x_second(chunk):
@@ -293,14 +311,14 @@
         x_copies[chunk, "r1"].wait_recv()
         sums[chunk, 1, :, top] = (join(chunk, 1, top) + first_in[chunk, 0].astype(F32)).astype(BF16)
         x_copies[chunk, "r2"] = remote(
-            sums.at[chunk, 1], second_in.at[chunk, 0], y_send.at[chunk, 0], y_recv.at[chunk, 0], right
+            sums.at[chunk, 1], second_in.at[chunk, 0], y_send.at[chunk, 0], y_recv.at[chunk, 0], here(right)
         )
         from_other[chunk, 3].wait_recv()
         sums[chunk, 3, :, top] = join(chunk, 3, top).astype(BF16)
         x_copies[chunk, "l1"].wait_recv()
         sums[chunk, 3, :, bottom] = (join(chunk, 3, bottom) + first_in[chunk, 1].astype(F32)).astype(BF16)
         x_copies[chunk, "l2"] = remote(
-            sums.at[chunk, 3], second_in.at[chunk, 1], y_send.at[chunk, 1], y_recv.at[chunk, 1], left
+            sums.at[chunk, 3], second_in.at[chunk, 1], y_send.at[chunk, 1], y_recv.at[chunk, 1], here(left)
         )
 
     z_copies = {}
@@ -319,15 +337,15 @@
             if near:
                 z_copies[chunk, near] = remote(
                     mixed.at[chunk, near], z_in.at[chunk, near], z_send.at[chunk, near], z_recv.at[chunk, near],
-                    to * 8 + x * 2 + c,
+                    here(to * 8 + x * 2 + c),
                 )
 
     def z_last(chunk):
-        total = mixed[chunk, 0].astype(F32)
+        value = mixed[chunk, 0].astype(F32)
         for near in (1, 2, 3):
             z_copies[chunk, near].wait_recv()
-            total = total + z_in[chunk, near].astype(F32)
-        out_ref[pl.ds(chunk * CR, CR), :] = total.astype(BF16)
+            value = value + z_in[chunk, near].astype(F32)
+        out_ref[pl.ds(chunk * CR, CR), :] = value.astype(BF16)
 
     from_z(0)
     spread_scales(gate_scales, gate_f32, 32)
@@ -353,62 +371,56 @@
     decode_piece(3, 3)
     from_far(2)
     from_core(0)
-
     for group in range(4):
         total[:, both_cols[group]] = product(0, group)
-
-    from_far(3)
     for z_at in range(4):
         decode_piece(2, z_at)
     from_core(1)
+    for group in range(4):
+        total[:, both_cols[group]] += product(1, group)
+    from_far(3)
     from_core(3)
-
     for group in range(4):
-        total[:, both_cols[group]] += product(1, group) + product(3, group)
-
+        total[:, both_cols[group]] += product(3, group)
     from_core(2)
-    for group in range(4):
-        both = total[:, both_cols[group]] + product(2, group)
-        for tile in range(2 * group, min(2 * group + 2, TILES)):
-            start = 256 * (tile - 2 * group)
-            gate, up = both[:, start : start + 128], both[:, start + 128 : start + 256]
-            value = gate / (1.0 + jnp.exp(-gate)) * up
-            hidden[:, :, pl.ds(128 * tile, 128)] = value.astype(BF16).reshape(16, 16, 128)
-
-        scatter(group)
-
+    for chunk in range(CHUNKS):
+        rows = pl.ds(chunk * CR, CR)
+        for group in range(4):
+            both = total[rows, both_cols[group]] + product(2, group, rows)
+            for tile in range(2 * group, min(2 * group + 2, TILES)):
+                start = 256 * (tile - 2 * group)
+                gate, up = both[:, start : start + 128], both[:, start + 128 : start + 256]
+                value = gate / (1.0 + jnp.exp(-gate)) * up
+                hidden[pl.ds(8 * chunk, 8), :, pl.ds(128 * tile, 128)] = value.astype(BF16).reshape(8, 16, 128)
+            scatter(chunk, group)
+
+    spread_scales(down_scales, down_f32, 7)
     factor_load.wait()
     for tile in range(TILES):
         cols = pl.ds(128 * tile, 128)
         ordered[:, cols] = jnp.dot(factor[:, cols], order, preferred_element_type=F32).astype(BF16)
-    spread_scales(down_scales, down_f32, 7)
     down_load.wait()
     decode_down(0, 8)
-    rotate_turn(0)
+    rotate(0)
     decode_down(8, 16)
-    rotate_turn(1)
-    back(0)
-    back(1)
-    first_part = jnp.dot(
-        rotated[:, :, pl.ds(0, 512)].reshape(ROWS, 512), ordered[pl.ds(0, 512), :], preferred_element_type=F32
-    )
-    back(2)
-    back(3)
-    whole = first_part + jnp.dot(
-        rotated[:, :, pl.ds(512, 384)].reshape(ROWS, 384), ordered[pl.ds(512, 384), :], preferred_element_type=F32
-    )
-    turned[...] = (whole * math.sqrt(TP)).astype(BF16)
-    down(2)
-    down(1)
+    rotate(1)
+    turn(0)
+    down(0, 2)
+    down(0, 1)
     x_first(0)
+    down(0, 3)
+    down(0, 0)
+    x_second(0)
+    turn(1)
+    down(1, 2)
+    down(1, 1)
     x_first(1)
-    down(3)
-    down(0)
-    x_second(0)
+    down(1, 3)
+    down(1, 0)
+    z_first(0)
     x_second(1)
-    z_first(0)
+    z_last(0)
     z_first(1)
-    z_last(0)
     z_last(1)
 
     for copy in waiting:
@@ -419,9 +431,12 @@
             def _():
                 sent = hidden.at[pl.ds(0, 16 - kept), :, group_cols[group]]
                 pltpu.make_async_copy(sent, sent, a_send.at[group]).wait()
-                if kept:
-                    sent = had_out.at[group // 2, pl.ds(0, TP - 1), :, pl.ds(0, group_width[group])]
-                    pltpu.make_async_copy(sent, sent, b_send.at[group // 2]).wait()
+    for chunk in range(CHUNKS):
+        for width in (256, 128):
+            @pl.when((my_group(chunk) == 3) if width == 128 else (my_group(chunk) < 3))
+            def _():
+                sent = had_out.at[chunk, pl.ds(0, TP - 1), :, pl.ds(0, width)]
+                pltpu.make_async_copy(sent, sent, b_send.at[chunk]).wait()
 
 
 def shards(tokens, gate_codes, gate_scales, up_codes, up_scales, local_factor, down_codes, down_scales):
@@ -460,9 +475,9 @@
             dma((48,)),
             dma((TP, 2)),
             dma((4,)),
-            dma((2,)),
-            dma((2,)),
-            dma((4,)),
+            dma((CHUNKS,)),
+            dma((CHUNKS,)),
+            dma((CHUNKS,)),
             dma((CHUNKS, 4)),
             dma((CHUNKS, 4)),
             dma((CHUNKS, 2)),

time: 71.6 us -> 73.1 us (1.021)
  Pallas kernels: 69.9 us -> 71.5 us
    pallas_call x1, Pallas kernels: 69.9 us -> 71.5 us  [shards(): pl.pallas_call(kernel, out_shape=jax.ShapeDtypeStruct((ROWS, 128), BF16),...]
where the time goes in v10:
time: 73.1 us; the launch traced here: 72.9 us
  Pallas kernels  71.5 us (98%)
  local copies, waits for them, and re-layouts  1.47 us (2%)
    pallas_call x1, Pallas kernels, shards(): pl.pallas_call(kernel, out_shape=jax.ShapeDtypeStruct((ROWS, 128), BF16),...  71.5 us
    unnamed x1, local copies, waits for them, and re-layouts  1.47 us

profile of v10, /device:TPU:16, one launch (start us, length us, event | category | flops | bytes accessed | tf_op | source)
XLA Modules:
  0.0 72.9 jit_solution(1829769124722653965)
XLA Ops:
  0.0 71.5 %feed_forward.1 = bf16[256,128]{1,0:T(8,128)(2,1)} custom-call(bf16[256,128]{1,0:T(8,128)(2,1)} %tok_in.1, bf16[32,896]{1,0:T(8,128)(2,1)} %gate_scales.1, bf16[32,896]{1,0:T(8,128)(2,1)} %up_scales.1, bf16[7,4096]{1,0:T(8,128)(2,1)} %down_scales.1, s32[1024,896]{1,0:T(8,128)} %gate_hbm.1, s32[1024,896]{1,0:T(8,128)} %up_hbm.1, bf16[896,896]{1,0:T(8,128)(2,1)} %factor_hbm.1, ...), custom_call_target="tpu_custom_call" | custom-call | tf_op jit(solution)/shard_map/feed_forward/pallas_call | solution.py:444
  71.5 1.5 %copy.10 = bf16[256,128]{1,0:T(8,128)(2,1)} copy(bf16[256,128]{1,0:T(8,128)(2,1)} %feed_forward.1) | data formatting | bytes 131072

commit v11 on v9

--- a/solution.py
+++ b/solution.py
@@ -74,12 +74,11 @@
                 pltpu.make_async_copy(gate_hbm.at[rows], gate_codes.at[rows], load_sem.at[first]),
                 pltpu.make_async_copy(up_hbm.at[rows], up_codes.at[rows], load_sem.at[first + 1]),
             ]
-            for copy in loads[shift, z_at]:
-                copy.start()
+            if not shift:
+                for copy in loads[shift, z_at]:
+                    copy.start(priority=1)
     factor_load = pltpu.make_async_copy(factor_hbm, factor, load_sem.at[32])
-    factor_load.start()
     down_load = pltpu.make_async_copy(down_hbm, down_codes, load_sem.at[33])
-    down_load.start()
 
     order = field_order()
 
@@ -139,14 +138,15 @@
         return z_of[near] * 8 + column(shift) * 2 + c
 
     def from_z(near):
+        block = at(near, 0)
         if near:
-            arrived(at(near, 0))
-        pass_on(at(near, 0), right)
-        pass_on(at(near, 0), left)
-        if not near:
+            arrived(block)
+        else:
             for peer in (1, 2, 3):
-                pass_on(me, at(peer, 0))
-        pass_on(at(near, 0), other)
+                pass_on(block, at(peer, 0))
+        pass_on(block, right)
+        pass_on(block, left)
+        pass_on(block, other)
 
     def from_x(near):
         block = at(near, 3)
@@ -334,6 +334,12 @@
         out_ref[pl.ds(chunk * CR, CR), :] = total.astype(BF16)
 
     from_z(0)
+    for shift in (1, 3, 2):
+        for z_at in range(4):
+            for copy in loads[shift, z_at]:
+                copy.start(priority=1)
+    factor_load.start(priority=1)
+    down_load.start(priority=1)
     for z_at in range(1, 4):
         decode_piece(0, z_at)
     from_z(1)

time: 71.6 us -> 71.7 us (level)
  no operation moved by 1% of the time
where the time goes in v11:
time: 71.7 us; the launch traced here: 71.4 us
  Pallas kernels  69.9 us (97%)
  local copies, waits for them, and re-layouts  1.47 us (2%)
    pallas_call x1, Pallas kernels, shards(): pl.pallas_call(kernel, out_shape=jax.ShapeDtypeStruct((ROWS, 128), BF16),...  69.9 us
    unnamed x1, local copies, waits for them, and re-layouts  1.47 us

profile of v11, /device:TPU:16, one launch (start us, length us, event | category | flops | bytes accessed | tf_op | source)
XLA Modules:
  0.0 71.4 jit_solution(17188452533003829379)
XLA Ops:
  0.0 69.9 %feed_forward.1 = bf16[256,128]{1,0:T(8,128)(2,1)} custom-call(bf16[256,128]{1,0:T(8,128)(2,1)} %tok_in.1, bf16[32,896]{1,0:T(8,128)(2,1)} %gate_scales.1, bf16[32,896]{1,0:T(8,128)(2,1)} %up_scales.1, bf16[7,4096]{1,0:T(8,128)(2,1)} %down_scales.1, s32[1024,896]{1,0:T(8,128)} %gate_hbm.1, s32[1024,896]{1,0:T(8,128)} %up_hbm.1, bf16[896,896]{1,0:T(8,128)(2,1)} %factor_hbm.1, ...), custom_call_target="tpu_custom_call" | custom-call | tf_op jit(solution)/shard_map/feed_forward/pallas_call | solution.py:437
  69.9 1.5 %copy.10 = bf16[256,128]{1,0:T(8,128)(2,1)} copy(bf16[256,128]{1,0:T(8,128)(2,1)} %feed_forward.1) | data formatting | bytes 131072

commit v12 on v11

--- a/solution.py
+++ b/solution.py
@@ -149,14 +149,13 @@
         pass_on(block, other)
 
     def from_x(near):
-        block = at(near, 3)
-        arrived(block)
-        pass_on(block, right, 0, ROWS // 2)
-        pass_on(block, other)
-        block = at(near, 1)
-        arrived(block)
-        pass_on(block, left, ROWS // 2, ROWS // 2)
-        pass_on(block, other)
+        before, after = at(near, 3), at(near, 1)
+        arrived(before)
+        pass_on(before, right, 0, ROWS // 2)
+        arrived(after)
+        pass_on(after, left, ROWS // 2, ROWS // 2)
+        pass_on(before, other)
+        pass_on(after, other)
 
     def from_far(near):
         block = at(near, 2)
@@ -407,9 +406,9 @@
     )
     turned[...] = (whole * math.sqrt(TP)).astype(BF16)
     down(2)
-    down(1)
     for chunk in range(CHUNKS):
         x_first(chunk)
+    down(1)
     down(3)
     down(0)
     for chunk in range(CHUNKS):

time: 71.7 us -> 71.7 us (level)
  no operation moved by 1% of the time
where the time goes in v12:
time: 71.7 us; the launch traced here: 71.4 us
  Pallas kernels  69.9 us (97%)
  local copies, waits for them, and re-layouts  1.47 us (2%)
    pallas_call x1, Pallas kernels, shards(): pl.pallas_call(kernel, out_shape=jax.ShapeDtypeStruct((ROWS, 128), BF16),...  69.9 us
    unnamed x1, local copies, waits for them, and re-layouts  1.47 us

profile of v12, /device:TPU:16, one launch (start us, length us, event | category | flops | bytes accessed | tf_op | source)
XLA Modules:
  0.0 71.4 jit_solution(2928307947934963317)
XLA Ops:
  0.0 69.9 %feed_forward.1 = bf16[256,128]{1,0:T(8,128)(2,1)} custom-call(bf16[256,128]{1,0:T(8,128)(2,1)} %tok_in.1, bf16[32,896]{1,0:T(8,128)(2,1)} %gate_scales.1, bf16[32,896]{1,0:T(8,128)(2,1)} %up_scales.1, bf16[7,4096]{1,0:T(8,128)(2,1)} %down_scales.1, s32[1024,896]{1,0:T(8,128)} %gate_hbm.1, s32[1024,896]{1,0:T(8,128)} %up_hbm.1, bf16[896,896]{1,0:T(8,128)(2,1)} %factor_hbm.1, ...), custom_call_target="tpu_custom_call" | custom-call | tf_op jit(solution)/shard_map/feed_forward/pallas_call | solution.py:436
  69.9 1.5 %copy.10 = bf16[256,128]{1,0:T(8,128)(2,1)} copy(bf16[256,128]{1,0:T(8,128)(2,1)} %feed_forward.1) | data formatting | bytes 131072
